TPU v7x, 256 devices: a whole 4x4x8 slice. The times are simulated.
256 devices in a mesh: dp: 32 (over z_hi, x, core), mp: 8 (over z_lo, y).
Axes of the slice: x: 4, y: 4, z: 8 (z_hi: 4, z_lo: 2; z = z_hi * 2 + z_lo), core: 2. Of those that a mesh axis runs over, the one named last changes fastest.
Arguments:
- tokens: bfloat16 [128, 64, 4096], P('dp', None, 'mp'), may hold values from -40 to 40
- groups: int32 [64, 128], P('dp'), may hold values from 0 to 127, each once within a row
- router: bfloat16 [4096, 64], P('mp'), may hold values from -0.5 to 0.5
- w_in: bfloat16 [65536, 4096], P(('mp', 'dp')), may hold values from -0.09375 to 0.09375
- w_out: bfloat16 [65536, 4096], P(('mp', 'dp')), may hold values from -0.75 to 0.75
- cotangent: bfloat16 [128, 64, 4096], P('dp', None, 'mp'), may hold values from -6 to 6
Outputs:
- mixed_out: bfloat16 [128, 64, 4096], P('dp', None, 'mp')
- tokens_grad: bfloat16 [128, 64, 4096], P('dp', None, 'mp')
- router_grad: float32 [4096, 64], P('mp')
- w_in_grad: bfloat16 [65536, 4096], P(('mp', 'dp'))
- w_out_grad: bfloat16 [65536, 4096], P(('mp', 'dp'))
Inputs may be any that keep to these rules, and one draw needn't show every extreme that they name: `groups`: each row is a permutation of the 128 sequences.
All inputs are finite; a program needn't handle non-finite values.
Results may differ from a plain program's by a relative error of at most 0.035.
Values may be sent and summed in bfloat16 or wider, within the bound.
A program may use at most 128 MiB of HBM per device.

v0:
```python
import jax
import jax.numpy as jnp
from jax import lax
from jax.sharding import PartitionSpec as P

GROUP = 32
SPLIT = 4


def group_rows(full_rows, groups):
    turned = jnp.swapaxes(full_rows, 0, 1)
    picked = jnp.take_along_axis(turned, groups[:, :, None], axis=1)
    return picked.reshape(-1, GROUP, full_rows.shape[2])


def ungroup_rows(grouped, groups):
    positions, seq_count = groups.shape
    flat_rows = grouped.reshape(positions, seq_count, grouped.shape[-1])
    row_ids = jnp.arange(positions, dtype=jnp.int32)[:, None]
    order_ids = jnp.broadcast_to(jnp.arange(seq_count, dtype=jnp.int32)[None, :], groups.shape)
    inverse = jnp.zeros_like(groups).at[row_ids, groups].set(order_ids)
    return jnp.swapaxes(jnp.take_along_axis(flat_rows, inverse[:, :, None], axis=1), 0, 1)


def send_owners(stacked):
    kinds, experts, local_groups, slice_width = stacked.shape
    n_model = lax.axis_size("mp")
    n_data = lax.axis_size("dp")
    per_owner = experts // n_model
    owned_rows = lax.all_to_all(stacked, "mp", split_axis=1, concat_axis=3, tiled=True)
    full_width = slice_width * n_model
    spread = jnp.broadcast_to(
        owned_rows[:, :, None], (kinds, per_owner, SPLIT, local_groups, full_width)
    )
    spread = spread.reshape(kinds, per_owner * SPLIT, local_groups, full_width)
    arrived = lax.all_to_all(spread, "dp", split_axis=1, concat_axis=1, tiled=True)
    return arrived.reshape(kinds, n_data * local_groups, slice_width * n_model)


def return_parts(parts, local_groups):
    kinds, all_groups, feat_width = parts.shape
    n_data = lax.axis_size("dp")
    per_owner = n_data // SPLIT
    sectioned = parts.reshape(kinds, n_data, local_groups, feat_width)
    arrived = lax.all_to_all(sectioned, "dp", split_axis=1, concat_axis=1, tiled=True)
    terms = arrived.reshape(kinds, per_owner, SPLIT, local_groups, feat_width)
    summed = jnp.sum(terms.astype(jnp.float32), axis=2).astype(jnp.bfloat16)
    result = lax.all_to_all(summed, "mp", split_axis=3, concat_axis=1, tiled=True)
    return result


def expert_forward(gathered, w_in, w_out):
    pre_act = jnp.einsum("gd,fd->gf", gathered, w_in, preferred_element_type=jnp.float32)
    active = jax.nn.silu(pre_act).astype(jnp.bfloat16)
    produced = jnp.einsum("gf,fd->gd", active, w_out, preferred_element_type=jnp.float32).astype(
        jnp.bfloat16
    )
    return (pre_act, active, produced)


def expert_backward(gathered, back_rows, pre_act, active, w_in, w_out):
    d_active = jnp.einsum("gd,fd->gf", back_rows, w_out, preferred_element_type=jnp.float32)
    grad_second = jnp.einsum(
        "gf,gd->fd", active, back_rows, preferred_element_type=jnp.float32
    ).astype(jnp.bfloat16)
    gate_sig = jax.nn.sigmoid(pre_act)
    d_pre = (d_active * gate_sig * (1.0 + pre_act * (1.0 - gate_sig))).astype(jnp.bfloat16)
    grad_first = jnp.einsum(
        "gf,gd->fd", d_pre, gathered, preferred_element_type=jnp.float32
    ).astype(jnp.bfloat16)
    d_mixed = jnp.einsum("gf,fd->gd", d_pre, w_in, preferred_element_type=jnp.float32).astype(
        jnp.bfloat16
    )
    return (grad_first, grad_second, d_mixed)


def per_device(tokens, groups, router, w_in, w_out, cotangent):
    tok_pos, cot_pos = (
        lax.all_to_all(tokens, "dp", split_axis=1, concat_axis=0, tiled=True),
        lax.all_to_all(cotangent, "dp", split_axis=1, concat_axis=0, tiled=True),
    )
    grouped_tok = group_rows(tok_pos, groups)
    grouped_cot = group_rows(cot_pos, groups)
    local_groups = grouped_tok.shape[0]
    logit_part = jnp.einsum("gtd,de->gte", grouped_tok, router, preferred_element_type=jnp.float32)
    logits = lax.psum(logit_part, "mp")
    weights = jax.nn.softmax(logits, axis=1)
    weight_bf = weights.astype(jnp.bfloat16)
    mixed_rows = jnp.einsum(
        "gte,gtd->egd", weight_bf, grouped_tok, preferred_element_type=jnp.float32
    ).astype(jnp.bfloat16)
    back_mix = jnp.einsum(
        "gte,gtd->egd", weight_bf, grouped_cot, preferred_element_type=jnp.float32
    ).astype(jnp.bfloat16)
    gathered = send_owners(mixed_rows[None])[0]
    pre_act, active, produced = expert_forward(gathered, w_in, w_out)
    outputs_y = return_parts(produced[None], local_groups)[0]
    back_rows = send_owners(back_mix[None])[0]
    grad_first, grad_second, d_mixed_part = expert_backward(
        gathered, back_rows, pre_act, active, w_in, w_out
    )
    d_mixed = return_parts(d_mixed_part[None], local_groups)[0]
    out_rows = jnp.einsum(
        "gte,egd->gtd", weight_bf, outputs_y, preferred_element_type=jnp.float32
    ).astype(jnp.bfloat16)
    weight_part = jnp.einsum(
        "gtd,egd->gte", grouped_cot, outputs_y, preferred_element_type=jnp.float32
    )
    weight_part = weight_part + jnp.einsum(
        "gtd,egd->gte", grouped_tok, d_mixed, preferred_element_type=jnp.float32
    )
    d_weight = lax.psum(weight_part.astype(jnp.bfloat16), "mp").astype(jnp.float32)
    d_logit = weights * (d_weight - jnp.sum(weights * d_weight, axis=1, keepdims=True))
    d_logit_bf = d_logit.astype(jnp.bfloat16)
    d_tokens = jnp.einsum("gte,egd->gtd", weight_bf, d_mixed, preferred_element_type=jnp.float32)
    d_tokens = d_tokens + jnp.einsum(
        "gte,de->gtd", d_logit_bf, router, preferred_element_type=jnp.float32
    )
    router_part = jnp.einsum(
        "gtd,gte->de", grouped_tok, d_logit_bf, preferred_element_type=jnp.float32
    )
    router_grad = lax.psum(router_part.astype(jnp.bfloat16), "dp").astype(jnp.float32)
    out_seq = ungroup_rows(out_rows, groups)
    grad_seq = ungroup_rows(d_tokens.astype(jnp.bfloat16), groups)
    mixed_out, tokens_grad = (
        lax.all_to_all(out_seq, "dp", split_axis=0, concat_axis=1, tiled=True),
        lax.all_to_all(grad_seq, "dp", split_axis=0, concat_axis=1, tiled=True),
    )
    return (mixed_out, tokens_grad, router_grad, grad_first, grad_second)


def solution(mesh):
    return jax.shard_map(
        per_device,
        mesh=mesh,
        in_specs=(
            P("dp", None, "mp"),
            P("dp", None),
            P("mp", None),
            P(("mp", "dp"), None),
            P(("mp", "dp"), None),
            P("dp", None, "mp"),
        ),
        out_specs=(
            P("dp", None, "mp"),
            P("dp", None, "mp"),
            P("mp", None),
            P(("mp", "dp"), None),
            P(("mp", "dp"), None),
        ),
        check_vma=False,
    )
```

profile of v0, /device:TPU:1, one launch (start us, length us, event | category | flops | bytes accessed | tf_op | source)
XLA Modules:
  0.0 799.1 jit_solution(9236841712147097207)
XLA Ops:
  9.2 12.6 %all-to-all-start = ((bf16[4,64,512]{2,0,1:T(4,128)(2,1)}), bf16[4,64,512]{2,0,1:T(4,128)(2,1)S(1)}, u32[]{:S(2)}, u32[]{:S(2)}) async-start(bf16[4,64,512]{2,0,1:T(4,128)(2,1)} %copy.44), calls=%async_computation | async-start | bytes 524288 | tf_op jit(solution)/shard_map/all_to_all | solution.py:79
  23.7 11.5 %all-to-all-done = bf16[4,64,512]{2,0,1:T(4,128)(2,1)S(1)} async-done(((bf16[4,64,512]{2,0,1:T(4,128)(2,1)}), bf16[4,64,512]{2,0,1:T(4,128)(2,1)S(1)}, u32[]{:S(2)}, u32[]{:S(2)}) %all-to-all-start) | async-done | bytes 262176 | tf_op jit(solution)/shard_map/all_to_all | solution.py:79
  39.2 12.8 %all-to-all-done.6 = bf16[4,64,512]{2,0,1:T(4,128)(2,1)S(1)} async-done(((bf16[4,64,512]{2,0,1:T(4,128)(2,1)}), bf16[4,64,512]{2,0,1:T(4,128)(2,1)S(1)}, u32[]{:S(2)}, u32[]{:S(2)}) %all-to-all-start.6) | async-done | bytes 262176 | tf_op jit(solution)/shard_map/all_to_all | solution.py:80
  57.4 69.5 %all-reduce.3.cloned.1.call-done = f32[8,32,64]{2,1,0:T(8,128)} async-done(((f32[8,32,64]{2,1,0:T(8,128)}), f32[8,32,64]{2,1,0:T(8,128)}) %all-reduce.3.cloned.1.call-update) | async-done | bytes 65552 | tf_op jit(solution)/shard_map/psum | solution.py:86
  152.8 16.6 %all-to-all-start.2 = ((bf16[1,32,8,4096]{3,2,0,1:T(8,128)(2,1)}), bf16[1,32,8,4096]{3,2,0,1:T(8,128)(2,1)}, u32[]{:S(2)}, u32[]{:S(2)}) async-start(bf16[1,32,8,4096]{3,2,0,1:T(8,128)(2,1)} %bitcast.168), calls=%async_computation.2 | async-start | bytes 4194304 | tf_op jit(solution)/shard_map/all_to_all | solution.py:36
  172.9 47.4 %all-to-all-done.2 = bf16[1,32,8,4096]{3,2,0,1:T(8,128)(2,1)} async-done(((bf16[1,32,8,4096]{3,2,0,1:T(8,128)(2,1)}), bf16[1,32,8,4096]{3,2,0,1:T(8,128)(2,1)}, u32[]{:S(2)}, u32[]{:S(2)}) %all-to-all-start.2) | async-done | bytes 2097184 | tf_op jit(solution)/shard_map/all_to_all | solution.py:36
  232.7 46.0 %all-to-all-done.8 = bf16[1,32,8,4096]{3,2,0,1:T(8,128)(2,1)} async-done(((bf16[1,32,8,4096]{3,2,0,1:T(8,128)(2,1)}), bf16[1,32,8,4096]{3,2,0,1:T(8,128)(2,1)}, u32[]{:S(2)}, u32[]{:S(2)}) %all-to-all-start.8) | async-done | bytes 2097184 | tf_op jit(solution)/shard_map/all_to_all | solution.py:36
  278.7 5.8 all-to-all-start.3
  289.1 44.3 %all-to-all-done.3 = bf16[1,32,8,4096]{3,2,0,1:T(8,128)(2,1)} async-done(((bf16[1,32,8,4096]{3,2,0,1:T(8,128)(2,1)}), bf16[1,32,8,4096]{3,2,0,1:T(8,128)(2,1)}, u32[]{:S(2)}, u32[]{:S(2)}) %all-to-all-start.3) | async-done | bytes 2097184 | tf_op jit(solution)/shard_map/all_to_all | solution.py:45
  333.4 7.6 all-to-all-start.9
  343.0 7.2 copy.49
  350.2 11.2 %reshape.108 = bf16[8,2,16384]{2,1,0:T(2,128)(2,1)} reshape(bf16[4096,1,8,8]{3,2,1,0:T(8,128)(2,1)} %bitcast.160) | data formatting | bytes 1048576
  361.3 28.7 %all-to-all-done.9 = bf16[1,32,8,4096]{3,2,0,1:T(8,128)(2,1)S(1)} async-done(((bf16[1,32,8,4096]{3,2,0,1:T(8,128)(2,1)}), bf16[1,32,8,4096]{3,2,0,1:T(8,128)(2,1)S(1)}, u32[]{:S(2)}, u32[]{:S(2)}) %all-to-all-start.9) | async-done | bytes 2097184 | tf_op jit(solution)/shard_map/all_to_all | solution.py:45
  395.1 11.4 %scatter_fusion = s32[2,128]{1,0:T(2,128)S(1)} fusion(s32[2,128]{1,0:T(2,128)S(1)} %broadcast.25, s32[256]{0:T(256)S(1)} %get-tuple-element.9, s32[256]{0:T(256)S(1)} %iota_bitcast_fusion), kind=kCustom, calls=%fused_computation.4 | custom fusion | bytes 5120 | tf_op jit(solution)/shard_map/scatter | solution.py:21
  408.5 7.2 copy.60
  415.7 11.2 %reshape.110 = bf16[8,2,16384]{2,1,0:T(2,128)(2,1)} reshape(bf16[4096,1,8,8]{3,2,1,0:T(8,128)(2,1)} %bitcast.161) | data formatting | bytes 1048576
  432.1 11.0 %reshape.109 = bf16[4096,1,8,8]{3,2,1,0:T(8,128)(2,1)} reshape(bf16[8,2,16384]{2,1,0:T(2,128)(2,1)S(1)} %all-to-all-done.4) | data formatting | bytes 1048576
  443.1 7.5 copy.65
  451.5 11.0 %reshape.111 = bf16[4096,1,8,8]{3,2,1,0:T(8,128)(2,1)} reshape(bf16[8,2,16384]{2,1,0:T(2,128)(2,1)S(1)} %all-to-all-done.10) | data formatting | bytes 1048576
  462.5 7.5 copy.66
  470.8 27.8 %psum.22 = bf16[8,32,64]{2,1,0:T(8,128)(2,1)S(1)} all-reduce(bf16[8,32,64]{2,1,0:T(8,128)(2,1)S(1)} %fusion.24), channel_id=1, replica_groups=mesh['dp'=32,'mp'=8] {'mp'}, use_global_device_ids=true, to_apply=%region_6.8 | all-reduce | flops 16384 | bytes 65536 | tf_op jit(solution)/shard_map/psum | solution.py:112
  504.7 13.7 %all-to-all-start.5 = ((bf16[128,2,512]{2,1,0:T(2,128)(2,1)}), bf16[128,2,512]{2,1,0:T(2,128)(2,1)S(1)}, u32[]{:S(2)}, u32[]{:S(2)}) async-start(bf16[128,2,512]{2,1,0:T(2,128)(2,1)} %get-tuple-element.7), calls=%async_computation.5 | async-start | bytes 524288 | tf_op jit(solution)/shard_map/all_to_all | solution.py:126
  522.1 9.2 %all-to-all-done.5 = bf16[128,2,512]{2,1,0:T(2,128)(2,1)S(1)} async-done(((bf16[128,2,512]{2,1,0:T(2,128)(2,1)}), bf16[128,2,512]{2,1,0:T(2,128)(2,1)S(1)}, u32[]{:S(2)}, u32[]{:S(2)}) %all-to-all-start.5) | async-done | bytes 262176 | tf_op jit(solution)/shard_map/all_to_all | solution.py:126
  540.7 248.0 %all-reduce.5.cloned.1.call-done = bf16[512,64]{0,1:T(8,128)(2,1)} async-done(((bf16[512,64]{0,1:T(8,128)(2,1)}), bf16[512,64]{0,1:T(8,128)(2,1)}) %all-reduce.5.cloned.1.call-update) | async-done | bytes 65552 | tf_op jit(solution)/shard_map/psum | solution.py:122
  (91 shorter events, 97.9 us)
Async XLA Ops:
  7.2 223.5 %copy-start = (bf16[256,4096]{1,0:T(8,128)(2,1)S(1)}, bf16[256,4096]{1,0:T(8,128)(2,1)}, u32[]{:S(2)}) copy-start(bf16[256,4096]{1,0:T(8,128)(2,1)} %param.12) | copy-start | bytes 6291460
  7.2 31.9 %copy-start.10 = (s32[2,128]{1,0:T(2,128)S(1)}, s32[2,128]{1,0:T(2,128)}, u32[]{:S(2)}) copy-start(s32[2,128]{1,0:T(2,128)} %param.9) | copy-start | bytes 3076
  9.2 26.0 %all-to-all-start = ((bf16[4,64,512]{2,0,1:T(4,128)(2,1)}), bf16[4,64,512]{2,0,1:T(4,128)(2,1)S(1)}, u32[]{:S(2)}, u32[]{:S(2)}) async-start(bf16[4,64,512]{2,0,1:T(4,128)(2,1)} %copy.44), calls=%async_computation | async-start | bytes 524288 | tf_op jit(solution)/shard_map/all_to_all | solution.py:79
  35.2 16.8 %all-to-all-start.6 = ((bf16[4,64,512]{2,0,1:T(4,128)(2,1)}), bf16[4,64,512]{2,0,1:T(4,128)(2,1)S(1)}, u32[]{:S(2)}, u32[]{:S(2)}) async-start(bf16[4,64,512]{2,0,1:T(4,128)(2,1)} %copy.55), calls=%async_computation.6 | async-start | bytes 524288 | tf_op jit(solution)/shard_map/all_to_all | solution.py:80
  39.0 87.9 %all-reduce.3.cloned.1.call-start = ((), (), s32[]{:S(2)}) async-start(), calls=%async_computation.12 | async-start | bytes 262144 | tf_op jit(solution)/shard_map/psum | solution.py:86
  54.3 2.2 copy-start.8
  128.0 6.4 copy-start.4
  129.4 10.6 %all-to-all-start.1 = ((bf16[1,64,8,512]{3,2,0,1:T(8,128)(2,1)}), bf16[1,64,8,512]{3,2,0,1:T(8,128)(2,1)S(1)}, u32[]{:S(2)}, u32[]{:S(2)}) async-start(bf16[1,64,8,512]{3,2,0,1:T(8,128)(2,1)} %copy.46), calls=%async_computation.1 | async-start | bytes 1048576 | tf_op jit(solution)/shard_map/all_to_all | solution.py:30
  140.0 11.3 %all-to-all-start.7 = ((bf16[1,64,8,512]{3,2,0,1:T(8,128)(2,1)}), bf16[1,64,8,512]{3,2,0,1:T(8,128)(2,1)}, u32[]{:S(2)}, u32[]{:S(2)}) async-start(bf16[1,64,8,512]{3,2,0,1:T(8,128)(2,1)} %copy.57), calls=%async_computation.7 | async-start | bytes 1048576 | tf_op jit(solution)/shard_map/all_to_all | solution.py:30
  152.8 67.5 %all-to-all-start.2 = ((bf16[1,32,8,4096]{3,2,0,1:T(8,128)(2,1)}), bf16[1,32,8,4096]{3,2,0,1:T(8,128)(2,1)}, u32[]{:S(2)}, u32[]{:S(2)}) async-start(bf16[1,32,8,4096]{3,2,0,1:T(8,128)(2,1)} %bitcast.168), calls=%async_computation.2 | async-start | bytes 4194304 | tf_op jit(solution)/shard_map/all_to_all | solution.py:36
  221.9 56.8 %all-to-all-start.8 = ((bf16[1,32,8,4096]{3,2,0,1:T(8,128)(2,1)}), bf16[1,32,8,4096]{3,2,0,1:T(8,128)(2,1)}, u32[]{:S(2)}, u32[]{:S(2)}) async-start(bf16[1,32,8,4096]{3,2,0,1:T(8,128)(2,1)} %bitcast.169), calls=%async_computation.8 | async-start | bytes 4194304 | tf_op jit(solution)/shard_map/all_to_all | solution.py:36
  278.7 54.7 %all-to-all-start.3 = ((bf16[1,32,8,4096]{3,2,0,1:T(8,128)(2,1)}), bf16[1,32,8,4096]{3,2,0,1:T(8,128)(2,1)}, u32[]{:S(2)}, u32[]{:S(2)}) async-start(bf16[1,32,8,4096]{3,2,0,1:T(8,128)(2,1)} %fusion.1), calls=%async_computation.3 | async-start | bytes 4194304 | tf_op jit(solution)/shard_map/all_to_all | solution.py:45
  284.5 2.5 copy-start.2
  333.4 56.6 %all-to-all-start.9 = ((bf16[1,32,8,4096]{3,2,0,1:T(8,128)(2,1)}), bf16[1,32,8,4096]{3,2,0,1:T(8,128)(2,1)S(1)}, u32[]{:S(2)}, u32[]{:S(2)}) async-start(bf16[1,32,8,4096]{3,2,0,1:T(8,128)(2,1)} %fusion.2), calls=%async_computation.9 | async-start | bytes 4194304 | tf_op jit(solution)/shard_map/all_to_all | solution.py:45
  390.0 5.0 copy-start.3
  390.1 36.8 %all-to-all-start.4 = ((bf16[8,2,16384]{2,1,0:T(2,128)(2,1)}), bf16[8,2,16384]{2,1,0:T(2,128)(2,1)S(1)}, u32[]{:S(2)}, u32[]{:S(2)}) async-start(bf16[8,2,16384]{2,1,0:T(2,128)(2,1)} %reshape.108), calls=%async_computation.4 | async-start | bytes 1048576 | tf_op jit(solution)/shard_map/all_to_all | solution.py:48
  426.8 24.7 %all-to-all-start.10 = ((bf16[8,2,16384]{2,1,0:T(2,128)(2,1)}), bf16[8,2,16384]{2,1,0:T(2,128)(2,1)S(1)}, u32[]{:S(2)}, u32[]{:S(2)}) async-start(bf16[8,2,16384]{2,1,0:T(2,128)(2,1)} %reshape.110), calls=%async_computation.10 | async-start | bytes 1048576 | tf_op jit(solution)/shard_map/all_to_all | solution.py:48
  443.1 7.5 copy-start.5
  469.9 28.8 %copy-start.9 = (bf16[512,64]{0,1:T(8,128)(2,1)S(1)}, bf16[512,64]{0,1:T(8,128)(2,1)}, u32[]{:S(2)}) copy-start(bf16[512,64]{0,1:T(8,128)(2,1)} %param.10) | copy-start | bytes 196612
  504.7 26.6 %all-to-all-start.5 = ((bf16[128,2,512]{2,1,0:T(2,128)(2,1)}), bf16[128,2,512]{2,1,0:T(2,128)(2,1)S(1)}, u32[]{:S(2)}, u32[]{:S(2)}) async-start(bf16[128,2,512]{2,1,0:T(2,128)(2,1)} %get-tuple-element.7), calls=%async_computation.5 | async-start | bytes 524288 | tf_op jit(solution)/shard_map/all_to_all | solution.py:126
  518.4 18.5 %copy-start.7 = (bf16[256,256]{1,0:T(8,128)(2,1)S(1)}, bf16[256,256]{1,0:T(8,128)(2,1)}, u32[]{:S(2)}) copy-start(bf16[256,256]{1,0:T(8,128)(2,1)} %copy-done.6) | copy-start | bytes 393220
  531.3 259.9 %all-to-all-start.11 = ((bf16[128,2,512]{2,1,0:T(2,128)(2,1)}), bf16[128,2,512]{2,1,0:T(2,128)(2,1)S(1)}, u32[]{:S(2)}, u32[]{:S(2)}) async-start(bf16[128,2,512]{2,1,0:T(2,128)(2,1)} %get-tuple-element.6), calls=%async_computation.11 | async-start | bytes 524288 | tf_op jit(solution)/shard_map/all_to_all | solution.py:127
  536.0 252.8 %all-reduce.5.cloned.1.call-start = ((), (), s32[]{:S(2)}) async-start(), calls=%async_computation.13 | async-start | bytes 131072 | tf_op jit(solution)/shard_map/psum | solution.py:122
  536.9 255.3 %copy-start.1 = (bf16[256,4096]{1,0:T(8,128)(2,1)S(1)}, bf16[256,4096]{1,0:T(8,128)(2,1)}, u32[]{:S(2)}) copy-start(bf16[256,4096]{1,0:T(8,128)(2,1)} %param.12) | copy-start | bytes 6291460
  (1 other events, 2.1 us)
Sparse Core Ops, SparseCore 0:
  57.6 69.3 all-reduce.2
  540.2 248.5 all-reduce.4
where the time goes:
time: 802 us; the launch traced here: 799 us
  waiting for transfers between devices  528 us (66%)
  local copies, waits for them, and re-layouts  111 us (14%)
  starting transfers between devices  88.3 us (11%)
  blocking collectives  27.8 us (3%)
  matrix products  21.4 us (3%)
  between operations  14.5 us (2%)
  other arithmetic  8.19 us (1%)
    psum x1, waiting for transfers between devices, per_device(): lax.psum(router_part.astype(jnp.bfloat16), 'dp').astype(jnp.float32)  248 us
    all_to_all x2, waiting for transfers between devices, send_owners(): lax.all_to_all(spread, 'dp', split_axis=1, concat_axis=1, tiled=True)  93.5 us
    all_to_all x2, waiting for transfers between devices, return_parts(): lax.all_to_all(sectioned, 'dp', split_axis=1, concat_axis=1, tiled=True)  73.1 us
    psum x1, waiting for transfers between devices, per_device(): logits = lax.psum(logit_part, 'mp')  69.5 us
    unnamed x28, local copies, waits for them, and re-layouts  48.2 us
    psum x1, blocking collectives, per_device(): lax.psum(weight_part.astype(jnp.bfloat16), 'mp').astype(jnp.float32)  27.8 us
    all_to_all x2, starting transfers between devices, send_owners(): lax.all_to_all(spread, 'dp', split_axis=1, concat_axis=1, tiled=True)  22.4 us
  transfers between devices with their start and end apart: 14, of which 11 were waited for; matrix products, arithmetic and copies ran while one was open for 13% of the time, Pallas kernels for 0%

commit v1 on v0

v1 whole, which is shorter than its diff:
```python
import jax
import jax.numpy as jnp
from jax import lax
from jax.experimental import pallas as pl
from jax.experimental.pallas import tpu as pltpu
from jax.sharding import PartitionSpec as P

MESH = pl.DeviceIdType.MESH
BF = jnp.bfloat16
F32 = jnp.float32
NDP = 32
NMP = 8
CH = 4

NT = (((1,), (1,)), ((), ()))
TN = (((0,), (0,)), ((), ()))


def dot(a, b):
    return jnp.dot(a, b, preferred_element_type=F32)


def dot_nt(a, b):
    return lax.dot_general(a, b, NT, preferred_element_type=F32)


def dot_tn(a, b):
    return lax.dot_general(a, b, TN, preferred_element_type=F32)


def iota(shape, dim):
    return lax.broadcasted_iota(jnp.int32, shape, dim)


def wait_bytes(view, sem):
    pltpu.make_async_copy(view, view, sem).wait()


(S_X, S_C, S_L, S_MIX, S_M, S_B, S_QSIB, S_QX, S_QF, S_BSIB, S_BX, S_BF) = range(12)
S_PSIB, S_PX, S_PA, S_DSIB, S_DX, S_DA, S_O, S_DW, S_DL, S_G, S_R, S_RG = range(12, 24)
N_SEND = 24
R_X, R_C, R_L, R_MIX, R_M, R_B, R_QSIB, R_QX, R_QF, R_BSIB, R_BX, R_BF = (0, 1, 2, 3, 4, 5, 6, 7, 11, 15, 16, 20)
R_PSIB, R_PX, R_PA, R_DSIB, R_DX, R_DA, R_O, R_DW, R_DL, R_G, R_R, R_RG = (24, 28, 32, 33, 37, 41, 42, 43, 44, 45, 46, 47)
N_RECV = 48


def kernel(tok, cot, grp, rt, w_in, w_out,
           o_mix, o_grad, o_router, o_win, o_wout,
           xs, cs, xin, cin, lsend, lin, mixsend, mixall, amat, mbuf, bbuf,
           g_fwd, g_back, xf, cf, wi, wo, pb, sb, xsum, xr, rb, pin,
           pb2, sb2, xsum2, xr2, rb2, din, osend, oin, gsend, gin,
           wlsend, wlin, dlsend, dlall, bacc, dtok, rsend, rin, rall, rsum, acc, gi, go,
           send, recv, wsem):
    me_p = lax.axis_index("dp")
    me_m = lax.axis_index("mp")
    p4 = me_p // 4
    q = me_p % 4
    u = me_m * 8 + p4
    sib = me_p + 1 - 2 * (me_p % 2)
    xnb = me_p + 2 - 4 * (q // 2)
    q_sib = q + 1 - 2 * (q % 2)
    q_x = q + 2 - 4 * (q // 2)
    q_d = q_sib + 2 - 4 * (q_sib // 2)

    def rcopy(src, dst, s, r, dev):
        return pltpu.make_async_remote_copy(
            src_ref=src, dst_ref=dst, send_sem=send.at[s], recv_sem=recv.at[r],
            device_id=dev, device_id_type=MESH)

    load_wi = pltpu.make_async_copy(w_in, wi, wsem.at[0])
    load_wo = pltpu.make_async_copy(w_out, wo, wsem.at[1])
    load_wi.start()
    load_wo.start()

    bar = pltpu.get_barrier_semaphore()

    def sig_row(k, c):
        pl.semaphore_signal(bar, inc=1, device_id=((me_p + k) % NDP, me_m), device_id_type=MESH)
        return c

    lax.fori_loop(1, NDP, sig_row, 0)

    def sig_class(k, c):
        col = (me_m + 1 + k // 8) % NMP
        pl.semaphore_signal(bar, inc=1, device_id=((k % 8) * 4 + q, col), device_id_type=MESH)
        return c

    lax.fori_loop(0, 56, sig_class, 0)

    r_i = iota((256, 256), 0)
    c_i = iota((256, 256), 1)
    src_row = ((r_i // 2) % 4) * 64 + (r_i // 8) * 2 + r_i % 2
    perm = (c_i == src_row).astype(F32).astype(BF)

    def blocks(ref, out):
        rows = ref[...].reshape(256, 512)
        for h in range(2):
            res = dot(perm, rows[:, h * 256:(h + 1) * 256])
            out[:, h * 8:(h + 1) * 8, :] = res.reshape(32, 8, 256).astype(BF)

    def send_row(src, dst, s, r):
        def body(k, c):
            peer = (me_p + k) % NDP
            rcopy(src.at[peer], dst.at[me_p], s, r, (peer, me_m)).start()
            return c
        lax.fori_loop(1, NDP, body, 0)

    def send_col(src, dst, s, r, spread):
        def body(k, c):
            peer = (me_m + k) % NMP
            part = src.at[peer] if spread else src
            rcopy(part, dst.at[me_m], s, r, (me_p, peer)).start()
            return c
        lax.fori_loop(1, NMP, body, 0)

    blocks(tok, xs)
    pl.semaphore_wait(bar, 31 + 56)
    send_row(xs, xin, S_X, R_X)
    blocks(cot, cs)
    send_row(cs, cin, S_C, R_C)
    xin[me_p] = xs[me_p]
    cin[me_p] = cs[me_p]

    t_i = iota((256, 128), 0)
    l_i = iota((256, 128), 1)
    order = jnp.where(t_i % 2 == 0, grp[0:1, :], grp[1:2, :])
    hit = (order == t_i // 2).astype(F32).astype(BF)
    g_i = iota((8, 128), 0)
    s_i = iota((8, 128), 1)
    pick = (s_i // 32 == g_i % 4).astype(F32).astype(BF)
    own_pos = (iota((8, 256), 1) % 2 == iota((8, 256), 0) // 4).astype(F32)
    m8 = dot_nt(pick, hit) * own_pos

    def half(ref, h, rows):
        return ref[:, h * 8:(h + 1) * 8, :].astype(F32).reshape(rows, ref.shape[-1]).astype(BF)

    wait_bytes(xin.at[pl.ds(0, 31)], recv.at[R_X])
    x0, x1 = half(xin, 0, 256), half(xin, 1, 256)
    r0, r1 = rt[:, 0:256], rt[:, 256:512]
    lsend[...] = (dot_nt(r0, x0) + dot_nt(r1, x1)).reshape(8, 8, 256)
    send_col(lsend, lin, S_L, R_L, True)
    lin[me_m] = lsend[me_m]
    wait_bytes(lin.at[pl.ds(0, 7)], recv.at[R_L])
    logit = jnp.sum(lin[...], axis=0)
    big = jnp.full((8, 256), -jnp.inf, F32)
    peak = jnp.zeros((8, 256), F32)
    for g in range(8):
        inside = jnp.broadcast_to(m8[g:g + 1, :] > 0.5, (8, 256))
        top = jnp.max(jnp.where(inside, logit, big), axis=1, keepdims=True)
        peak = jnp.where(inside, top, peak)
    ex = jnp.exp(logit - peak)
    den = jnp.zeros((8, 256), F32)
    for g in range(8):
        mask = m8[g:g + 1, :]
        den = den + mask * jnp.sum(ex * mask, axis=1, keepdims=True)
    mix_own = ex / den
    mixsend[0:8, :] = mix_own[:, 0:128].astype(BF)
    mixsend[8:16, :] = mix_own[:, 128:256].astype(BF)
    send_col(mixsend, mixall, S_MIX, R_MIX, False)
    mixall[me_m] = mixsend[...]
    wait_bytes(mixall.at[pl.ds(0, 7)], recv.at[R_MIX])

    spread = (iota((512, 64), 0) // 8 == iota((512, 64), 1)).astype(F32).astype(BF)
    for h in range(2):
        wide = dot(spread, half(mixall, h, 64)).reshape(64, 8, 128)
        sel = wide * m8[:, h * 128:(h + 1) * 128][None]
        amat[:, h * 128:(h + 1) * 128] = sel.reshape(512, 128).astype(BF)

    def send_class(src, dst, s, r):
        def body(k, c):
            v = (u + k) % 64
            rcopy(src.at[v], dst, s, r, ((v % 8) * 4 + q, v // 8)).start()
            return c
        lax.fori_loop(1, 64, body, 0)

    def mixing(rows, buf, dst, s, r):
        for h in range(2):
            res = dot(amat[...], rows[h])
            buf[:, h * 8:(h + 1) * 8, :] = res.reshape(64, 8, 256).astype(BF)
        send_class(buf, dst.at[q, u], s, r)
        dst[q, u] = buf[u]

    mixing((x0, x1), mbuf, g_fwd, S_M, R_M)
    wait_bytes(cin.at[pl.ds(0, 31)], recv.at[R_C])
    mixing((half(cin, 0, 256), half(cin, 1, 256)), bbuf, g_back, S_B, R_B)

    def quad_start(g, r_own, s_sib, r_sib, s_x, r_x):
        wait_bytes(g.at[0, pl.ds(0, 63)], recv.at[r_own])

        def body(j, c):
            part = g.at[q, pl.ds(j * 16, 16)]
            rcopy(part, part, s_x, r_x + j, (xnb, me_m)).start()
            return c
        lax.fori_loop(0, CH, body, 0)
        rcopy(g.at[q], g.at[q], s_sib, r_sib, (sib, me_m)).start()

    def quad_forward(g, r_x, s_f, r_f):
        def body(j, c):
            part = g.at[q_x, pl.ds(j * 16, 16)]
            wait_bytes(part, recv.at[r_x + j])
            rcopy(part, part, s_f, r_f + j, (sib, me_m)).start()
            return c
        lax.fori_loop(0, CH, body, 0)

    def quad_done(g, r_sib, r_f):
        wait_bytes(g.at[q_sib], recv.at[r_sib])

        def body(j, c):
            wait_bytes(g.at[q_d, pl.ds(j * 16, 16)], recv.at[r_f + j])
            return c
        lax.fori_loop(0, CH, body, 0)

    def project(g, flat, w):
        acc[...] = jnp.zeros((256, 256), F32)

        def body(m, c):
            for h in range(2):
                col = pl.multiple_of(m * 512 + h * 256, 256)
                part = g[:, pl.ds(m * 8, 8), h * 8:(h + 1) * 8, :].astype(F32).reshape(256, 256).astype(BF)
                flat[:, pl.ds(col, 256)] = part
                acc[...] += dot_nt(part, w[:, pl.ds(col, 256)])
            return c
        lax.fori_loop(0, NMP, body, 0)
        return acc[...]

    def parts(rows, w, buf, landing, s, r):
        def chunk(j, c):
            jj = (me_m // 2 + j) % CH

            def one(i, c2):
                m = jj * 2 + i
                for h in range(2):
                    col = pl.multiple_of(m * 512 + h * 256, 256)
                    res = dot(rows, w[:, pl.ds(col, 256)])
                    buf[:, pl.ds(m * 8, 8), h * 8:(h + 1) * 8, :] = res.reshape(4, 8, 8, 256).astype(BF)
                return c2
            lax.fori_loop(0, 2, one, 0)
            span = pl.ds(jj * 16, 16)
            rcopy(buf.at[q_d, span], landing.at[1, span], s, r + j, (sib, me_m)).start()
            rcopy(buf.at[q_sib, span], landing.at[0, span], s, r + j, (sib, me_m)).start()
            return c
        lax.fori_loop(0, CH, chunk, 0)

    def pair_sums(buf, landing, out, far, r_sib, s, r):
        def chunk(j, c):
            jj = (me_m // 2 + j) % CH
            span = pl.ds(jj * 16, 16)
            wait_bytes(landing.at[pl.ds(0, 2), span], recv.at[r_sib + j])
            out[span] = (buf[q_x, span].astype(F32) + landing[1, span].astype(F32)).astype(BF)
            rcopy(out.at[span], far.at[span], s, r + j, (xnb, me_m)).start()
            return c
        lax.fori_loop(0, CH, chunk, 0)

    def totals(buf, landing, far, out, home, r_x, s, r):
        def finish(jj, j):
            span = pl.ds(jj * 16, 16)
            wait_bytes(far.at[span], recv.at[r_x + j])
            out[span] = (buf[q, span].astype(F32) + landing[0, span].astype(F32)
                         + far[span].astype(F32)).astype(BF)

        def post(v):
            rcopy(out.at[v], home.at[u], s, r, ((v % 8) * 4 + q, v // 8)).start()

        first = me_m // 2
        finish(first, 0)
        w = u % 16

        def near(k, c):
            post(first * 16 + (w + k) % 16)
            return c
        lax.fori_loop(1, 16, near, 0)
        home[u] = out[u]

        def chunk(j, c):
            jj = (first + j) % CH
            finish(jj, j)

            def each(k, c2):
                post(jj * 16 + (w + k) % 16)
                return c2
            lax.fori_loop(0, 16, each, 0)
            return c
        lax.fori_loop(1, CH, chunk, 0)

    quad_start(g_fwd, R_M, S_QSIB, R_QSIB, S_QX, R_QX)
    quad_forward(g_fwd, R_QX, S_QF, R_QF)
    quad_start(g_back, R_B, S_BSIB, R_BSIB, S_BX, R_BX)
    load_wi.wait()
    load_wo.wait()
    quad_done(g_fwd, R_QSIB, R_QF)
    pre = project(g_fwd, xf, wi)
    sig = 1.0 / (1.0 + jnp.exp(-pre))
    act_f = pre * sig
    slope = sig * (1.0 + pre * (1.0 - sig))
    dtok[:, 0:256] = slope
    active = act_f.astype(BF)
    parts(active, wo, pb, sb, S_PSIB, R_PSIB)
    quad_forward(g_back, R_BX, S_BF, R_BF)
    pair_sums(pb, sb, xsum, xr, R_PSIB, S_PX, R_PX)
    quad_done(g_back, R_BSIB, R_BF)
    d_pre_f = project(g_back, cf, wo) * dtok[:, 0:256]
    d_pre = d_pre_f.astype(BF)
    parts(d_pre, wi, pb2, sb2, S_DSIB, R_DSIB)
    totals(pb, sb, xr, rb, pin, R_PX, S_PA, R_PA)
    pair_sums(pb2, sb2, xsum2, xr2, R_DSIB, S_DX, R_DX)
    active_t = act_f.T.astype(BF)
    d_pre_t = d_pre_f.T.astype(BF)

    def weight_grads(m, c):
        col = pl.ds(pl.multiple_of(m * 512, 512), 512)
        go[:, col] = dot(active_t, cf[:, col]).astype(BF)
        gi[:, col] = dot(d_pre_t, xf[:, col]).astype(BF)
        return c
    lax.fori_loop(0, NMP, weight_grads, 0)
    store_wi = pltpu.make_async_copy(gi, o_win, wsem.at[2])
    store_wo = pltpu.make_async_copy(go, o_wout, wsem.at[3])
    store_wi.start()
    store_wo.start()
    totals(pb2, sb2, xr2, rb2, din, R_DX, S_DA, R_DA)

    wait_bytes(pin.at[pl.ds(0, 63)], recv.at[R_PA])
    for h in range(2):
        rows = half(pin, h, 512)
        res = dot_tn(amat[...], rows)
        osend[:, h * 8:(h + 1) * 8, :] = res.reshape(32, 8, 256).astype(BF)
        part = dot_nt(rows, half(cin, h, 256))
        if h == 0:
            bacc[...] = part
        else:
            bacc[...] += part
    send_row(osend, oin, S_O, R_O)
    oin[me_p] = osend[me_p]

    wait_bytes(din.at[pl.ds(0, 63)], recv.at[R_DA])
    for h in range(2):
        bacc[...] += dot_nt(half(din, h, 512), half(xin, h, 256))
    wlsend[...] = jnp.sum(bacc[...].reshape(64, 8, 256) * m8[None], axis=1).reshape(8, 8, 256)
    send_col(wlsend, wlin, S_DW, R_DW, True)
    wlin[me_m] = wlsend[me_m]
    for h in range(2):
        dtok[:, h * 256:(h + 1) * 256] = dot_tn(amat[...], half(din, h, 512))
    wait_bytes(wlin.at[pl.ds(0, 7)], recv.at[R_DW])
    d_weight = jnp.sum(wlin[...], axis=0)
    prod = mix_own * d_weight
    mean = jnp.zeros((8, 256), F32)
    for g in range(8):
        mask = m8[g:g + 1, :]
        mean = mean + mask * jnp.sum(prod * mask, axis=1, keepdims=True)
    d_logit = mix_own * (d_weight - mean)
    dlsend[0:8, :] = d_logit[:, 0:128].astype(BF)
    dlsend[8:16, :] = d_logit[:, 128:256].astype(BF)
    send_col(dlsend, dlall, S_DL, R_DL, False)
    dlall[me_m] = dlsend[...]
    wait_bytes(dlall.at[pl.ds(0, 7)], recv.at[R_DL])
    dl = jnp.concatenate([half(dlall, 0, 64), half(dlall, 1, 64)], axis=1)
    for h in range(2):
        res = dtok[:, h * 256:(h + 1) * 256] + dot_tn(dl, rt[:, h * 256:(h + 1) * 256])
        gsend[:, h * 8:(h + 1) * 8, :] = res.reshape(32, 8, 256).astype(BF)
    send_row(gsend, gin, S_G, R_G)
    gin[me_p] = gsend[me_p]
    for h in range(2):
        part = dot(dl, half(xin, h, 256))
        for k in range(2):
            tile = part[:, k * 128:(k + 1) * 128].reshape(8, 8, 128)
            for e in range(8):
                rsend[e * 4 + h * 2 + k] = tile[e]
    send_row(rsend, rin, S_R, R_R)
    rin[me_p] = rsend[me_p]
    wait_bytes(rin.at[pl.ds(0, 31)], recv.at[R_R])
    rsum[...] = jnp.sum(rin[...], axis=0)

    def share(k, c):
        peer = (me_p + k) % NDP
        rcopy(rsum, rall.at[me_p], S_RG, R_RG, (peer, me_m)).start()
        return c
    lax.fori_loop(1, NDP, share, 0)
    rall[me_p] = rsum[...]

    def place(src, out):
        for h in range(2):
            res = dot_tn(perm, half(src, h, 256)).astype(BF)
            out[:, :, h * 256:(h + 1) * 256] = res.reshape(4, 64, 256)

    wait_bytes(oin.at[pl.ds(0, 31)], recv.at[R_O])
    place(oin, o_mix)
    wait_bytes(gin.at[pl.ds(0, 31)], recv.at[R_G])
    place(gin, o_grad)
    wait_bytes(rall.at[pl.ds(0, 31)], recv.at[R_RG])
    for e in range(8):
        for k in range(4):
            o_router[e * 8:(e + 1) * 8, k * 128:(k + 1) * 128] = rall[e * 4 + k]

    for view, s in (
        (xs.at[pl.ds(0, 31)], S_X), (cs.at[pl.ds(0, 31)], S_C), (lin.at[pl.ds(0, 7)], S_L),
        (mixall.at[pl.ds(0, 7)], S_MIX), (mbuf.at[pl.ds(0, 63)], S_M), (bbuf.at[pl.ds(0, 63)], S_B),
        (g_fwd.at[0], S_QSIB), (g_fwd.at[0], S_QX), (g_fwd.at[0], S_QF),
        (g_back.at[0], S_BSIB), (g_back.at[0], S_BX), (g_back.at[0], S_BF),
        (sb, S_PSIB), (xsum, S_PX), (rb.at[pl.ds(0, 63)], S_PA),
        (sb2, S_DSIB), (xsum2, S_DX), (rb2.at[pl.ds(0, 63)], S_DA),
        (osend.at[pl.ds(0, 31)], S_O), (wlin.at[pl.ds(0, 7)], S_DW), (dlall.at[pl.ds(0, 7)], S_DL),
        (gsend.at[pl.ds(0, 31)], S_G), (rsend.at[pl.ds(0, 31)], S_R), (rall.at[pl.ds(0, 31)], S_RG),
    ):
        wait_bytes(view, send.at[s])
    store_wi.wait()
    store_wo.wait()


def per_device(tokens, groups, router, w_in, w_out, cotangent):
    vm = lambda shape, dt=BF: pltpu.VMEM(shape, dt)
    blk32, blk64 = (32, 16, 256), (64, 16, 256)
    scratch = [
        vm(blk32), vm(blk32), vm(blk32), vm(blk32),
        vm((8, 8, 256), F32), vm((8, 8, 256), F32), vm((16, 128)), vm((8, 16, 128)), vm((512, 256)),
        vm(blk64), vm(blk64),
        vm((4,) + blk64), vm((4,) + blk64), vm((256, 4096)), vm((256, 4096)),
        vm((256, 4096)), vm((256, 4096)),
        vm((4,) + blk64), vm((2,) + blk64), vm(blk64), vm(blk64), vm(blk64), vm(blk64),
        vm((4,) + blk64), vm((2,) + blk64), vm(blk64), vm(blk64), vm(blk64), vm(blk64),
        vm(blk32), vm(blk32), vm(blk32), vm(blk32),
        vm((8, 8, 256), F32), vm((8, 8, 256), F32), vm((16, 128)), vm((8, 16, 128)), vm((512, 256), F32), vm((256, 512), F32),
        vm((32, 8, 128), F32), vm((32, 8, 128), F32), vm((32, 8, 128), F32), vm((8, 128), F32),
        vm((256, 256), F32), vm((256, 4096)), vm((256, 4096)),
        pltpu.SemaphoreType.DMA((N_SEND,)), pltpu.SemaphoreType.DMA((N_RECV,)),
        pltpu.SemaphoreType.DMA((4,)),
    ]
    in_vmem = pl.BlockSpec(memory_space=pltpu.VMEM)
    anywhere = pl.BlockSpec(memory_space=pl.ANY)
    mixed_out, tokens_grad, router_t, g_in, g_out = pl.pallas_call(
        kernel,
        out_shape=(
            jax.ShapeDtypeStruct((4, 64, 512), BF),
            jax.ShapeDtypeStruct((4, 64, 512), BF),
            jax.ShapeDtypeStruct((64, 512), F32),
            jax.ShapeDtypeStruct((256, 4096), BF),
            jax.ShapeDtypeStruct((256, 4096), BF),
        ),
        in_specs=[in_vmem, in_vmem, in_vmem, in_vmem, anywhere, anywhere],
        out_specs=[in_vmem, in_vmem, in_vmem, anywhere, anywhere],
        scratch_shapes=scratch,
        compiler_params=pltpu.CompilerParams(
            collective_id=0, has_side_effects=True, vmem_limit_bytes=56 * 1024 * 1024),
        cost_estimate=pl.CostEstimate(flops=4 * 10**9, bytes_accessed=10**7, transcendentals=10**5),
    )(tokens, cotangent, groups, router.T, w_in, w_out)
    return mixed_out, tokens_grad, router_t.T, g_in, g_out


def solution(mesh):
    return jax.shard_map(
        per_device,
        mesh=mesh,
        in_specs=(
            P("dp", None, "mp"),
            P("dp", None),
            P("mp", None),
            P(("mp", "dp"), None),
            P(("mp", "dp"), None),
            P("dp", None, "mp"),
        ),
        out_specs=(
            P("dp", None, "mp"),
            P("dp", None, "mp"),
            P("mp", None),
            P(("mp", "dp"), None),
            P(("mp", "dp"), None),
        ),
        check_vma=False,
    )
```

time: 802 us -> 158 us (0.20)
  waiting for transfers between devices: 528 us -> 0 us
  Pallas kernels: 0 us -> 147 us
  local copies, waits for them, and re-layouts: 111 us -> 9.51 us
  starting transfers between devices: 88.3 us -> 0 us
  blocking collectives: 27.8 us -> 0 us
  matrix products: 21.4 us -> 0 us
  between operations: 14.5 us -> 0.64 us
  other arithmetic: 8.19 us -> 0 us
    psum x2 -> x0, waiting for transfers between devices: 318 us -> none  [the longest x1 248 us: per_device(): lax.psum(router_part.astype(jnp.bfloat16), 'dp').astype(jnp.float32)]
    all_to_all x12 -> x0, waiting for transfers between devices: 210 us -> none  [the longest x2 93.5 us: send_owners(): lax.all_to_all(spread, 'dp', split_axis=1, concat_axis=1, tiled=True)]
    pallas_call x0 -> x1, Pallas kernels: none -> 147 us  [per_device(): pl.pallas_call(kernel, out_shape=(jax.ShapeDtypeStruct((4, 64, 512), BF),...]
    all_to_all x12 -> x0, starting transfers between devices: 88.2 us -> none  [the longest x2 22.4 us: send_owners(): lax.all_to_all(spread, 'dp', split_axis=1, concat_axis=1, tiled=True)]
    unnamed x28 -> x7, local copies, waits for them, and re-layouts: 48.2 us -> 9.51 us
    psum x1 -> x0, blocking collectives: 27.8 us -> none  [per_device(): lax.psum(weight_part.astype(jnp.bfloat16), 'mp').astype(jnp.float32)]
    dot_general x15 -> x0, matrix products: 21.4 us -> none  [the longest x1 3.79 us: expert_backward(): jnp.einsum('gf,gd->fd', d_pre, gathered, preferred_element_type=jnp.float32)]
    all_to_all x12 -> x0, local copies, waits for them, and re-layouts: 20.5 us -> none  [the longest x2 15 us: return_parts(): lax.all_to_all(summed, 'mp', split_axis=3, concat_axis=1, tiled=True)]
  transfers between devices with their start and end apart: 14 -> 0, of which waited for: 11 -> 0; matrix products, arithmetic and copies ran while one was open for 13% -> 0% of each run, Pallas kernels for 0% -> 0%
where the time goes in v1:
time: 158 us; the launch traced here: 157 us
  Pallas kernels  147 us (93%)
  local copies, waits for them, and re-layouts  9.51 us (6%)
    pallas_call x1, Pallas kernels, per_device(): pl.pallas_call(kernel, out_shape=(jax.ShapeDtypeStruct((4, 64, 512), BF),...  147 us
    unnamed x7, local copies, waits for them, and re-layouts  9.51 us

profile of v1, /device:TPU:1, one launch (start us, length us, event | category | flops | bytes accessed | tf_op | source)
XLA Modules:
  0.0 157.4 jit_solution(8654898184100385083)
XLA Ops:
  0.6 147.3 %shard_map.101 = (bf16[4,64,512]{2,1,0:T(8,128)(2,1)}, bf16[4,64,512]{2,1,0:T(8,128)(2,1)}, f32[64,512]{1,0:T(8,128)}, bf16[256,4096]{1,0:T(8,128)(2,1)}, bf16[256,4096]{1,0:T(8,128)(2,1)}) custom-call(bf16[4,64,512]{2,1,0:T(8,128)(2,1)} %tok.1, bf16[4,64,512]{2,1,0:T(8,128)(2,1)} %cot.1, s32[2,128]{1,0:T(2,128)} %grp.1, bf16[64,512]{1,0:T(8,128)(2,1)} %bitcast.3, ...), custom_call_target="tpu_custom_call" | custom-call | flops 4000000000 | bytes 10000000 | tf_op jit(solution)/shard_map/pallas_call | solution.py:428
  147.9 1.7 %copy.16 = bf16[4,64,512]{2,1,0:T(8,128)(2,1)} copy(bf16[4,64,512]{2,1,0:T(8,128)(2,1)} %get-tuple-element.20) | data formatting | bytes 524288
  149.6 1.7 %copy.17 = bf16[4,64,512]{2,1,0:T(8,128)(2,1)} copy(bf16[4,64,512]{2,1,0:T(8,128)(2,1)} %get-tuple-element.21) | data formatting | bytes 524288
  151.3 1.6 copy.18
  152.8 0.0 copy-start
  152.8 3.3 %copy.19 = bf16[256,4096]{1,0:T(8,128)(2,1)} copy(bf16[256,4096]{1,0:T(8,128)(2,1)} %get-tuple-element.23) | data formatting | bytes 4194304
  156.1 0.0 copy-done
  156.1 1.3 copy.20
Async XLA Ops:
  152.8 3.3 %copy-start = (bf16[256,4096]{1,0:T(8,128)(2,1)S(1)}, bf16[256,4096]{1,0:T(8,128)(2,1)}, u32[]{:S(2)}) copy-start(bf16[256,4096]{1,0:T(8,128)(2,1)} %get-tuple-element.24) | copy-start | bytes 6291460

commit v2 on v1

--- a/solution.py
+++ b/solution.py
@@ -39,9 +39,9 @@
 (S_X, S_C, S_L, S_MIX, S_M, S_B, S_QSIB, S_QX, S_QF, S_BSIB, S_BX, S_BF) = range(12)
 S_PSIB, S_PX, S_PA, S_DSIB, S_DX, S_DA, S_O, S_DW, S_DL, S_G, S_R, S_RG = range(12, 24)
 N_SEND = 24
-R_X, R_C, R_L, R_MIX, R_M, R_B, R_QSIB, R_QX, R_QF, R_BSIB, R_BX, R_BF = (0, 1, 2, 3, 4, 5, 6, 7, 11, 15, 16, 20)
-R_PSIB, R_PX, R_PA, R_DSIB, R_DX, R_DA, R_O, R_DW, R_DL, R_G, R_R, R_RG = (24, 28, 32, 33, 37, 41, 42, 43, 44, 45, 46, 47)
-N_RECV = 48
+R_X, R_C, R_L, R_MIX, R_PA, R_DA, R_O, R_DW, R_DL, R_G, R_R, R_RG = range(12)
+(R_M, R_B, R_QSIB, R_QX, R_QF, R_BSIB, R_BX, R_BF, R_PSIB, R_PX, R_DSIB, R_DX) = range(12, 60, 4)
+N_RECV = 60
 
 
 def kernel(tok, cot, grp, rt, w_in, w_out,
@@ -62,6 +62,12 @@
     q_x = q + 2 - 4 * (q // 2)
     q_d = q_sib + 2 - 4 * (q_sib // 2)
 
+    def near_q(quad):
+        return ((q // 2 + quad + p4) % 2) * 2 + q % 2
+
+    def near_dp(quad):
+        return quad * 4 + near_q(quad)
+
     def rcopy(src, dst, s, r, dev):
         return pltpu.make_async_remote_copy(
             src_ref=src, dst_ref=dst, send_sem=send.at[s], recv_sem=recv.at[r],
@@ -82,7 +88,7 @@
 
     def sig_class(k, c):
         col = (me_m + 1 + k // 8) % NMP
-        pl.semaphore_signal(bar, inc=1, device_id=((k % 8) * 4 + q, col), device_id_type=MESH)
+        pl.semaphore_signal(bar, inc=1, device_id=(near_dp(k % 8), col), device_id_type=MESH)
         return c
 
     lax.fori_loop(0, 56, sig_class, 0)
@@ -166,62 +172,53 @@
         sel = wide * m8[:, h * 128:(h + 1) * 128][None]
         amat[:, h * 128:(h + 1) * 128] = sel.reshape(512, 128).astype(BF)
 
-    def send_class(src, dst, s, r):
-        def body(k, c):
-            v = (u + k) % 64
-            rcopy(src.at[v], dst, s, r, ((v % 8) * 4 + q, v // 8)).start()
-            return c
-        lax.fori_loop(1, 64, body, 0)
-
-    def mixing(rows, buf, dst, s, r):
+    def mixing(rows, buf, dst):
         for h in range(2):
             res = dot(amat[...], rows[h])
             buf[:, h * 8:(h + 1) * 8, :] = res.reshape(64, 8, 256).astype(BF)
-        send_class(buf, dst.at[q, u], s, r)
         dst[q, u] = buf[u]
 
-    mixing((x0, x1), mbuf, g_fwd, S_M, R_M)
-    wait_bytes(cin.at[pl.ds(0, 31)], recv.at[R_C])
-    mixing((half(cin, 0, 256), half(cin, 1, 256)), bbuf, g_back, S_B, R_B)
-
-    def quad_start(g, r_own, s_sib, r_sib, s_x, r_x):
-        wait_bytes(g.at[0, pl.ds(0, 63)], recv.at[r_own])
-
-        def body(j, c):
-            part = g.at[q, pl.ds(j * 16, 16)]
+    def send_chunk(src, dst, s, r, j):
+        def body(k, c):
+            m = (me_m + 2 * j + k // 8) % NMP
+            quad = (p4 + k) % 8
+            rcopy(src.at[m * 8 + quad], dst.at[near_q(quad), u], s, r + j, (near_dp(quad), m)).start()
+            return c
+        lax.fori_loop(1 if j == 0 else 0, 16, body, 0)
+
+    def chunk_spans(j):
+        return [pl.ds(((me_m - 2 * j - i + NMP) % NMP) * 8, 8) for i in range(2)]
+
+    def quad_chunk(g, r_own, s_sib, r_sib, s_x, r_x, j):
+        wait_bytes(g.at[0, pl.ds(0, 15 if j == 0 else 16)], recv.at[r_own + j])
+        for span in chunk_spans(j):
+            part = g.at[q, span]
             rcopy(part, part, s_x, r_x + j, (xnb, me_m)).start()
-            return c
-        lax.fori_loop(0, CH, body, 0)
-        rcopy(g.at[q], g.at[q], s_sib, r_sib, (sib, me_m)).start()
-
-    def quad_forward(g, r_x, s_f, r_f):
-        def body(j, c):
-            part = g.at[q_x, pl.ds(j * 16, 16)]
-            wait_bytes(part, recv.at[r_x + j])
+        for span in chunk_spans(j):
+            part = g.at[q, span]
+            rcopy(part, part, s_sib, r_sib + j, (sib, me_m)).start()
+
+    def quad_forward(g, r_x, s_f, r_f, j):
+        wait_bytes(g.at[0, pl.ds(0, 16)], recv.at[r_x + j])
+        for span in chunk_spans(j):
+            part = g.at[q_x, span]
             rcopy(part, part, s_f, r_f + j, (sib, me_m)).start()
-            return c
-        lax.fori_loop(0, CH, body, 0)
-
-    def quad_done(g, r_sib, r_f):
-        wait_bytes(g.at[q_sib], recv.at[r_sib])
-
-        def body(j, c):
-            wait_bytes(g.at[q_d, pl.ds(j * 16, 16)], recv.at[r_f + j])
-            return c
-        lax.fori_loop(0, CH, body, 0)
-
-    def project(g, flat, w):
-        acc[...] = jnp.zeros((256, 256), F32)
-
-        def body(m, c):
+
+    def project(g, flat, w, r_sib, r_f, j):
+        wait_bytes(g.at[0, pl.ds(0, 16)], recv.at[r_sib + j])
+        wait_bytes(g.at[0, pl.ds(0, 16)], recv.at[r_f + j])
+        if j == 0:
+            acc[...] = jnp.zeros((256, 256), F32)
+
+        def body(i, c):
+            m = (me_m - 2 * j - i + NMP) % NMP
             for h in range(2):
                 col = pl.multiple_of(m * 512 + h * 256, 256)
                 part = g[:, pl.ds(m * 8, 8), h * 8:(h + 1) * 8, :].astype(F32).reshape(256, 256).astype(BF)
                 flat[:, pl.ds(col, 256)] = part
                 acc[...] += dot_nt(part, w[:, pl.ds(col, 256)])
             return c
-        lax.fori_loop(0, NMP, body, 0)
-        return acc[...]
+        lax.fori_loop(0, 2, body, 0)
 
     def parts(rows, w, buf, landing, s, r):
         def chunk(j, c):
@@ -259,7 +256,7 @@
                          + far[span].astype(F32)).astype(BF)
 
         def post(v):
-            rcopy(out.at[v], home.at[u], s, r, ((v % 8) * 4 + q, v // 8)).start()
+            rcopy(out.at[v], home.at[u], s, r, (near_dp(v % 8), v // 8)).start()
 
         first = me_m // 2
         finish(first, 0)
@@ -282,27 +279,39 @@
             return c
         lax.fori_loop(1, CH, chunk, 0)
 
-    quad_start(g_fwd, R_M, S_QSIB, R_QSIB, S_QX, R_QX)
-    quad_forward(g_fwd, R_QX, S_QF, R_QF)
-    quad_start(g_back, R_B, S_BSIB, R_BSIB, S_BX, R_BX)
+    mixing((x0, x1), mbuf, g_fwd)
+    for j in range(CH):
+        send_chunk(mbuf, g_fwd, S_M, R_M, j)
+    wait_bytes(cin.at[pl.ds(0, 31)], recv.at[R_C])
+    mixing((half(cin, 0, 256), half(cin, 1, 256)), bbuf, g_back)
+    for j in range(CH):
+        quad_chunk(g_fwd, R_M, S_QSIB, R_QSIB, S_QX, R_QX, j)
+        send_chunk(bbuf, g_back, S_B, R_B, j)
+        if j > 0:
+            quad_forward(g_fwd, R_QX, S_QF, R_QF, j - 1)
+    quad_forward(g_fwd, R_QX, S_QF, R_QF, CH - 1)
     load_wi.wait()
     load_wo.wait()
-    quad_done(g_fwd, R_QSIB, R_QF)
-    pre = project(g_fwd, xf, wi)
+    for j in range(CH):
+        quad_chunk(g_back, R_B, S_BSIB, R_BSIB, S_BX, R_BX, j)
+        project(g_fwd, xf, wi, R_QSIB, R_QF, j)
+    pre = acc[...]
     sig = 1.0 / (1.0 + jnp.exp(-pre))
     act_f = pre * sig
     slope = sig * (1.0 + pre * (1.0 - sig))
     dtok[:, 0:256] = slope
     active = act_f.astype(BF)
     parts(active, wo, pb, sb, S_PSIB, R_PSIB)
-    quad_forward(g_back, R_BX, S_BF, R_BF)
     pair_sums(pb, sb, xsum, xr, R_PSIB, S_PX, R_PX)
-    quad_done(g_back, R_BSIB, R_BF)
-    d_pre_f = project(g_back, cf, wo) * dtok[:, 0:256]
+    for j in range(CH):
+        quad_forward(g_back, R_BX, S_BF, R_BF, j)
+    for j in range(CH):
+        project(g_back, cf, wo, R_BSIB, R_BF, j)
+    d_pre_f = acc[...] * dtok[:, 0:256]
     d_pre = d_pre_f.astype(BF)
     parts(d_pre, wi, pb2, sb2, S_DSIB, R_DSIB)
+    pair_sums(pb2, sb2, xsum2, xr2, R_DSIB, S_DX, R_DX)
     totals(pb, sb, xr, rb, pin, R_PX, S_PA, R_PA)
-    pair_sums(pb2, sb2, xsum2, xr2, R_DSIB, S_DX, R_DX)
     active_t = act_f.T.astype(BF)
     d_pre_t = d_pre_f.T.astype(BF)
 
@@ -354,11 +363,6 @@
     wait_bytes(dlall.at[pl.ds(0, 7)], recv.at[R_DL])
     dl = jnp.concatenate([half(dlall, 0, 64), half(dlall, 1, 64)], axis=1)
     for h in range(2):
-        res = dtok[:, h * 256:(h + 1) * 256] + dot_tn(dl, rt[:, h * 256:(h + 1) * 256])
-        gsend[:, h * 8:(h + 1) * 8, :] = res.reshape(32, 8, 256).astype(BF)
-    send_row(gsend, gin, S_G, R_G)
-    gin[me_p] = gsend[me_p]
-    for h in range(2):
         part = dot(dl, half(xin, h, 256))
         for k in range(2):
             tile = part[:, k * 128:(k + 1) * 128].reshape(8, 8, 128)
@@ -366,6 +370,18 @@
                 rsend[e * 4 + h * 2 + k] = tile[e]
     send_row(rsend, rin, S_R, R_R)
     rin[me_p] = rsend[me_p]
+    for h in range(2):
+        res = dtok[:, h * 256:(h + 1) * 256] + dot_tn(dl, rt[:, h * 256:(h + 1) * 256])
+        gsend[:, h * 8:(h + 1) * 8, :] = res.reshape(32, 8, 256).astype(BF)
+    send_row(gsend, gin, S_G, R_G)
+    gin[me_p] = gsend[me_p]
+    def place(src, out):
+        for h in range(2):
+            res = dot_tn(perm, half(src, h, 256)).astype(BF)
+            out[:, :, h * 256:(h + 1) * 256] = res.reshape(4, 64, 256)
+
+    wait_bytes(oin.at[pl.ds(0, 31)], recv.at[R_O])
+    place(oin, o_mix)
     wait_bytes(rin.at[pl.ds(0, 31)], recv.at[R_R])
     rsum[...] = jnp.sum(rin[...], axis=0)
 
@@ -376,13 +392,6 @@
     lax.fori_loop(1, NDP, share, 0)
     rall[me_p] = rsum[...]
 
-    def place(src, out):
-        for h in range(2):
-            res = dot_tn(perm, half(src, h, 256)).astype(BF)
-            out[:, :, h * 256:(h + 1) * 256] = res.reshape(4, 64, 256)
-
-    wait_bytes(oin.at[pl.ds(0, 31)], recv.at[R_O])
-    place(oin, o_mix)
     wait_bytes(gin.at[pl.ds(0, 31)], recv.at[R_G])
     place(gin, o_grad)
     wait_bytes(rall.at[pl.ds(0, 31)], recv.at[R_RG])
@@ -403,6 +412,16 @@
         wait_bytes(view, send.at[s])
     store_wi.wait()
     store_wo.wait()
+
+
+def copy_out(*refs):
+    count = len(refs) // 2
+    sem = refs[-1]
+    moves = [pltpu.make_async_copy(refs[i], refs[count + i], sem.at[i]) for i in range(count)]
+    for move in moves:
+        move.start()
+    for move in moves:
+        move.wait()
 
 
 def per_device(tokens, groups, router, w_in, w_out, cotangent):
@@ -425,15 +444,16 @@
     ]
     in_vmem = pl.BlockSpec(memory_space=pltpu.VMEM)
     anywhere = pl.BlockSpec(memory_space=pl.ANY)
-    mixed_out, tokens_grad, router_t, g_in, g_out = pl.pallas_call(
+    shapes = (
+        jax.ShapeDtypeStruct((4, 64, 512), BF),
+        jax.ShapeDtypeStruct((4, 64, 512), BF),
+        jax.ShapeDtypeStruct((64, 512), F32),
+        jax.ShapeDtypeStruct((256, 4096), BF),
+        jax.ShapeDtypeStruct((256, 4096), BF),
+    )
+    results = pl.pallas_call(
         kernel,
-        out_shape=(
-            jax.ShapeDtypeStruct((4, 64, 512), BF),
-            jax.ShapeDtypeStruct((4, 64, 512), BF),
-            jax.ShapeDtypeStruct((64, 512), F32),
-            jax.ShapeDtypeStruct((256, 4096), BF),
-            jax.ShapeDtypeStruct((256, 4096), BF),
-        ),
+        out_shape=shapes,
         in_specs=[in_vmem, in_vmem, in_vmem, in_vmem, anywhere, anywhere],
         out_specs=[in_vmem, in_vmem, in_vmem, anywhere, anywhere],
         scratch_shapes=scratch,
@@ -441,6 +461,13 @@
             collective_id=0, has_side_effects=True, vmem_limit_bytes=56 * 1024 * 1024),
         cost_estimate=pl.CostEstimate(flops=4 * 10**9, bytes_accessed=10**7, transcendentals=10**5),
     )(tokens, cotangent, groups, router.T, w_in, w_out)
+    mixed_out, tokens_grad, router_t, g_in, g_out = pl.pallas_call(
+        copy_out,
+        out_shape=shapes,
+        in_specs=[anywhere] * 5,
+        out_specs=[anywhere] * 5,
+        scratch_shapes=[pltpu.SemaphoreType.DMA((5,))],
+    )(*results)
     return mixed_out, tokens_grad, router_t.T, g_in, g_out
 
 

time: 158 us -> 280 us (1.77)
  Pallas kernels: 147 us -> 280 us
  local copies, waits for them, and re-layouts: 9.51 us -> 0 us
    pallas_call x1 -> x2, Pallas kernels: 147 us -> 280 us  [the longest x1 148 us: per_device(): pl.pallas_call(copy_out, out_shape=shapes, in_specs=[anywhere] * 5, out_s...]
    unnamed x7 -> x0, local copies, waits for them, and re-layouts: 9.51 us -> none
where the time goes in v2:
time: 280 us
  Pallas kernels  280 us (100%)
    pallas_call x1, Pallas kernels, per_device(): pl.pallas_call(copy_out, out_shape=shapes, in_specs=[anywhere] * 5, out_s...  148 us
    pallas_call x1, Pallas kernels, per_device(): pl.pallas_call(kernel, out_shape=shapes, in_specs=[in_vmem, in_vmem, in_v...  132 us

profile of v2, /device:TPU:1, one launch (start us, length us, event | category | flops | bytes accessed | tf_op | source)
XLA Modules:
  0.0 280.3 jit_solution(13794293094160302356)
XLA Ops:
  0.6 131.6 %shard_map.101 = (bf16[4,64,512]{2,1,0:T(8,128)(2,1)}, bf16[4,64,512]{2,1,0:T(8,128)(2,1)}, f32[64,512]{1,0:T(8,128)}, bf16[256,4096]{1,0:T(8,128)(2,1)}, bf16[256,4096]{1,0:T(8,128)(2,1)}) custom-call(bf16[4,64,512]{2,1,0:T(8,128)(2,1)} %tok.1, bf16[4,64,512]{2,1,0:T(8,128)(2,1)} %cot.1, s32[2,128]{1,0:T(2,128)} %grp.1, bf16[64,512]{1,0:T(8,128)(2,1)} %bitcast.3, ...), custom_call_target="tpu_custom_call" | custom-call | flops 4000000000 | bytes 10000000 | tf_op jit(solution)/shard_map/pallas_call | solution.py:454
  132.3 148.1 %shard_map.102 = (bf16[4,64,512]{2,1,0:T(8,128)(2,1)}, bf16[4,64,512]{2,1,0:T(8,128)(2,1)}, f32[64,512]{1,0:T(8,128)}, bf16[256,4096]{1,0:T(8,128)(2,1)}, bf16[256,4096]{1,0:T(8,128)(2,1)}) custom-call(bf16[4,64,512]{2,1,0:T(8,128)(2,1)} %get-tuple-element.15.refs_0_, bf16[4,64,512]{2,1,0:T(8,128)(2,1)} %get-tuple-element.16.refs_1_, ...), custom_call_target="tpu_custom_call" | custom-call | tf_op jit(solution)/shard_map/pallas_call | solution.py:464

commit v3 on v2

--- a/solution.py
+++ b/solution.py
@@ -49,7 +49,7 @@
            xs, cs, xin, cin, lsend, lin, mixsend, mixall, amat, mbuf, bbuf,
            g_fwd, g_back, xf, cf, wi, wo, pb, sb, xsum, xr, rb, pin,
            pb2, sb2, xsum2, xr2, rb2, din, osend, oin, gsend, gin,
-           wlsend, wlin, dlsend, dlall, bacc, dtok, rsend, rin, rall, rsum, acc, gi, go,
+           wlsend, wlin, dlsend, dlall, bacc, dtok, rsend, rin, rall, rsum, acc,
            send, recv, wsem):
     me_p = lax.axis_index("dp")
     me_m = lax.axis_index("mp")
@@ -86,12 +86,11 @@
 
     lax.fori_loop(1, NDP, sig_row, 0)
 
-    def sig_class(k, c):
-        col = (me_m + 1 + k // 8) % NMP
-        pl.semaphore_signal(bar, inc=1, device_id=(near_dp(k % 8), col), device_id_type=MESH)
+    def sig_col(k, c):
+        pl.semaphore_signal(bar, inc=1, device_id=(me_p, (me_m + k) % NMP), device_id_type=MESH)
         return c
 
-    lax.fori_loop(0, 56, sig_class, 0)
+    lax.fori_loop(1, NMP, sig_col, 0)
 
     r_i = iota((256, 256), 0)
     c_i = iota((256, 256), 1)
@@ -120,10 +119,9 @@
         lax.fori_loop(1, NMP, body, 0)
 
     blocks(tok, xs)
-    pl.semaphore_wait(bar, 31 + 56)
+    pl.semaphore_wait(bar, 31 + 7)
     send_row(xs, xin, S_X, R_X)
     blocks(cot, cs)
-    send_row(cs, cin, S_C, R_C)
     xin[me_p] = xs[me_p]
     cin[me_p] = cs[me_p]
 
@@ -145,6 +143,7 @@
     r0, r1 = rt[:, 0:256], rt[:, 256:512]
     lsend[...] = (dot_nt(r0, x0) + dot_nt(r1, x1)).reshape(8, 8, 256)
     send_col(lsend, lin, S_L, R_L, True)
+    send_row(cs, cin, S_C, R_C)
     lin[me_m] = lsend[me_m]
     wait_bytes(lin.at[pl.ds(0, 7)], recv.at[R_L])
     logit = jnp.sum(lin[...], axis=0)
@@ -248,36 +247,20 @@
             return c
         lax.fori_loop(0, CH, chunk, 0)
 
-    def totals(buf, landing, far, out, home, r_x, s, r):
-        def finish(jj, j):
-            span = pl.ds(jj * 16, 16)
-            wait_bytes(far.at[span], recv.at[r_x + j])
-            out[span] = (buf[q, span].astype(F32) + landing[0, span].astype(F32)
-                         + far[span].astype(F32)).astype(BF)
-
-        def post(v):
+    def total_chunk(buf, landing, far, out, home, r_x, s, r, j):
+        jj = (me_m // 2 + j) % CH
+        span = pl.ds(jj * 16, 16)
+        wait_bytes(far.at[span], recv.at[r_x + j])
+        out[span] = (buf[q, span].astype(F32) + landing[0, span].astype(F32)
+                     + far[span].astype(F32)).astype(BF)
+
+        def post(k, c):
+            v = jj * 16 + (u + k) % 16
             rcopy(out.at[v], home.at[u], s, r, (near_dp(v % 8), v // 8)).start()
-
-        first = me_m // 2
-        finish(first, 0)
-        w = u % 16
-
-        def near(k, c):
-            post(first * 16 + (w + k) % 16)
-            return c
-        lax.fori_loop(1, 16, near, 0)
-        home[u] = out[u]
-
-        def chunk(j, c):
-            jj = (first + j) % CH
-            finish(jj, j)
-
-            def each(k, c2):
-                post(jj * 16 + (w + k) % 16)
-                return c2
-            lax.fori_loop(0, 16, each, 0)
-            return c
-        lax.fori_loop(1, CH, chunk, 0)
+            return c
+        lax.fori_loop(1 if j == 0 else 0, 16, post, 0)
+        if j == 0:
+            home[u] = out[u]
 
     mixing((x0, x1), mbuf, g_fwd)
     for j in range(CH):
@@ -309,23 +292,25 @@
         project(g_back, cf, wo, R_BSIB, R_BF, j)
     d_pre_f = acc[...] * dtok[:, 0:256]
     d_pre = d_pre_f.astype(BF)
+    first = (pb, sb, xr, rb, pin, R_PX, S_PA, R_PA)
+    second = (pb2, sb2, xr2, rb2, din, R_DX, S_DA, R_DA)
+    total_chunk(*first, 0)
+    total_chunk(*first, 1)
     parts(d_pre, wi, pb2, sb2, S_DSIB, R_DSIB)
+    total_chunk(*first, 2)
     pair_sums(pb2, sb2, xsum2, xr2, R_DSIB, S_DX, R_DX)
-    totals(pb, sb, xr, rb, pin, R_PX, S_PA, R_PA)
+    total_chunk(*first, 3)
     active_t = act_f.T.astype(BF)
     d_pre_t = d_pre_f.T.astype(BF)
 
     def weight_grads(m, c):
         col = pl.ds(pl.multiple_of(m * 512, 512), 512)
-        go[:, col] = dot(active_t, cf[:, col]).astype(BF)
-        gi[:, col] = dot(d_pre_t, xf[:, col]).astype(BF)
+        o_wout[:, col] = dot(active_t, cf[:, col]).astype(BF)
+        o_win[:, col] = dot(d_pre_t, xf[:, col]).astype(BF)
         return c
     lax.fori_loop(0, NMP, weight_grads, 0)
-    store_wi = pltpu.make_async_copy(gi, o_win, wsem.at[2])
-    store_wo = pltpu.make_async_copy(go, o_wout, wsem.at[3])
-    store_wi.start()
-    store_wo.start()
-    totals(pb2, sb2, xr2, rb2, din, R_DX, S_DA, R_DA)
+    for j in range(CH):
+        total_chunk(*second, j)
 
     wait_bytes(pin.at[pl.ds(0, 63)], recv.at[R_PA])
     for h in range(2):
@@ -410,14 +395,11 @@
         (gsend.at[pl.ds(0, 31)], S_G), (rsend.at[pl.ds(0, 31)], S_R), (rall.at[pl.ds(0, 31)], S_RG),
     ):
         wait_bytes(view, send.at[s])
-    store_wi.wait()
-    store_wo.wait()
 
 
 def copy_out(*refs):
-    count = len(refs) // 2
-    sem = refs[-1]
-    moves = [pltpu.make_async_copy(refs[i], refs[count + i], sem.at[i]) for i in range(count)]
+    sems = refs[-1]
+    moves = [pltpu.make_async_copy(refs[i], refs[5 + i], sems.at[i]) for i in (3, 4, 0, 1, 2)]
     for move in moves:
         move.start()
     for move in moves:
@@ -438,12 +420,13 @@
         vm(blk32), vm(blk32), vm(blk32), vm(blk32),
         vm((8, 8, 256), F32), vm((8, 8, 256), F32), vm((16, 128)), vm((8, 16, 128)), vm((512, 256), F32), vm((256, 512), F32),
         vm((32, 8, 128), F32), vm((32, 8, 128), F32), vm((32, 8, 128), F32), vm((8, 128), F32),
-        vm((256, 256), F32), vm((256, 4096)), vm((256, 4096)),
+        vm((256, 256), F32),
         pltpu.SemaphoreType.DMA((N_SEND,)), pltpu.SemaphoreType.DMA((N_RECV,)),
-        pltpu.SemaphoreType.DMA((4,)),
+        pltpu.SemaphoreType.DMA((2,)),
     ]
     in_vmem = pl.BlockSpec(memory_space=pltpu.VMEM)
     anywhere = pl.BlockSpec(memory_space=pl.ANY)
+    in_hbm = pl.BlockSpec(memory_space=pltpu.HBM)
     shapes = (
         jax.ShapeDtypeStruct((4, 64, 512), BF),
         jax.ShapeDtypeStruct((4, 64, 512), BF),
@@ -454,11 +437,11 @@
     results = pl.pallas_call(
         kernel,
         out_shape=shapes,
-        in_specs=[in_vmem, in_vmem, in_vmem, in_vmem, anywhere, anywhere],
-        out_specs=[in_vmem, in_vmem, in_vmem, anywhere, anywhere],
+        in_specs=[in_vmem, in_vmem, in_vmem, in_vmem, in_hbm, in_hbm],
+        out_specs=[in_vmem] * 5,
         scratch_shapes=scratch,
         compiler_params=pltpu.CompilerParams(
-            collective_id=0, has_side_effects=True, vmem_limit_bytes=56 * 1024 * 1024),
+            collective_id=0, has_side_effects=True, vmem_limit_bytes=48 * 1024 * 1024),
         cost_estimate=pl.CostEstimate(flops=4 * 10**9, bytes_accessed=10**7, transcendentals=10**5),
     )(tokens, cotangent, groups, router.T, w_in, w_out)
     mixed_out, tokens_grad, router_t, g_in, g_out = pl.pallas_call(
@@ -467,6 +450,7 @@
         in_specs=[anywhere] * 5,
         out_specs=[anywhere] * 5,
         scratch_shapes=[pltpu.SemaphoreType.DMA((5,))],
+        compiler_params=pltpu.CompilerParams(vmem_limit_bytes=2 * 1024 * 1024),
     )(*results)
     return mixed_out, tokens_grad, router_t.T, g_in, g_out
 

time: 280 us -> 131 us (0.47)
  Pallas kernels: 280 us -> 127 us
  local copies, waits for them, and re-layouts: 0 us -> 3.41 us
    pallas_call x1, Pallas kernels: 148 us -> 2.24 us  [per_device(): pl.pallas_call(copy_out, out_shape=shapes, in_specs=[anywhere] * 5, out_s...]
    pallas_call x1, Pallas kernels: 132 us -> 125 us  [per_device(): pl.pallas_call(kernel, out_shape=shapes, in_specs=[in_vmem, in_vmem, in_v...]
    unnamed x0 -> x8, local copies, waits for them, and re-layouts: none -> 3.41 us
where the time goes in v3:
time: 131 us
  Pallas kernels  127 us (97%)
  local copies, waits for them, and re-layouts  3.41 us (3%)
    pallas_call x1, Pallas kernels, per_device(): pl.pallas_call(kernel, out_shape=shapes, in_specs=[in_vmem, in_vmem, in_v...  125 us
    unnamed x8, local copies, waits for them, and re-layouts  3.41 us

profile of v3, /device:TPU:1, one launch (start us, length us, event | category | flops | bytes accessed | tf_op | source)
XLA Modules:
  0.0 131.1 jit_solution(2800220322080259126)
XLA Ops:
  0.6 0.0 copy-start
  0.6 0.9 copy-done
  1.6 0.0 copy-start.1
  1.6 0.9 copy-done.1
  2.5 0.0 copy-start.2
  2.5 0.8 copy-done.2
  3.4 0.0 copy-start.3
  3.4 0.7 copy-done.3
  4.1 124.8 %shard_map.101 = (bf16[4,64,512]{2,1,0:T(8,128)(2,1)S(1)}, bf16[4,64,512]{2,1,0:T(8,128)(2,1)S(1)}, f32[64,512]{1,0:T(8,128)S(1)}, bf16[256,4096]{1,0:T(8,128)(2,1)S(1)}, bf16[256,4096]{1,0:T(8,128)(2,1)S(1)}) custom-call(bf16[4,64,512]{2,1,0:T(8,128)(2,1)S(1)} %copy-done, bf16[4,64,512]{2,1,0:T(8,128)(2,1)S(1)} %copy-done.1, s32[2,128]{1,0:T(2,128)S(1)} %copy-done.3, ...), custom_call_target="tpu_custom_call" | custom-call | flops 4000000000 | bytes 10000000 | tf_op jit(solution)/shard_map/pallas_call | solution.py:437
  128.9 2.2 %shard_map.102 = (bf16[4,64,512]{2,1,0:T(8,128)(2,1)}, bf16[4,64,512]{2,1,0:T(8,128)(2,1)}, f32[64,512]{1,0:T(8,128)}, bf16[256,4096]{1,0:T(8,128)(2,1)}, bf16[256,4096]{1,0:T(8,128)(2,1)}) custom-call(bf16[4,64,512]{2,1,0:T(8,128)(2,1)S(1)} %get-tuple-element.15.refs_0_, bf16[4,64,512]{2,1,0:T(8,128)(2,1)S(1)} %get-tuple-element.16.refs_1_, ...), custom_call_target="tpu_custom_call" | custom-call | tf_op jit(solution)/shard_map/pallas_call | solution.py:447
Async XLA Ops:
  0.6 1.0 copy-start
  1.6 0.9 copy-start.1
  2.5 0.8 copy-start.2
  3.4 0.7 copy-start.3

commit v4 on v3

--- a/solution.py
+++ b/solution.py
@@ -37,19 +37,20 @@
 
 
 (S_X, S_C, S_L, S_MIX, S_M, S_B, S_QSIB, S_QX, S_QF, S_BSIB, S_BX, S_BF) = range(12)
-S_PSIB, S_PX, S_PA, S_DSIB, S_DX, S_DA, S_O, S_DW, S_DL, S_G, S_R, S_RG = range(12, 24)
-N_SEND = 24
+S_PSIB, S_PX, S_PA, S_DSIB, S_DX, S_DA, S_O, S_DW, S_DL, S_G, S_R, S_RG, S_T = range(12, 25)
+N_SEND = 25
 R_X, R_C, R_L, R_MIX, R_PA, R_DA, R_O, R_DW, R_DL, R_G, R_R, R_RG = range(12)
 (R_M, R_B, R_QSIB, R_QX, R_QF, R_BSIB, R_BX, R_BF, R_PSIB, R_PX, R_DSIB, R_DX) = range(12, 60, 4)
-N_RECV = 60
-
-
-def kernel(tok, cot, grp, rt, w_in, w_out,
+R_T = 60
+N_RECV = 61
+
+
+def kernel(tok_in, cot_in, grp_in, rt_in, w_in, w_out,
            o_mix, o_grad, o_router, o_win, o_wout,
-           xs, cs, xin, cin, lsend, lin, mixsend, mixall, amat, mbuf, bbuf,
+           tok, cot, grp, rt, xs, cs, xin, cin, lsend, lin, mixsend, mixall, amat, mbuf, bbuf,
            g_fwd, g_back, xf, cf, wi, wo, pb, sb, xsum, xr, rb, pin,
            pb2, sb2, xsum2, xr2, rb2, din, osend, oin, gsend, gin,
-           wlsend, wlin, dlsend, dlall, bacc, dtok, rsend, rin, rall, rsum, acc,
+           wlsend, wlin, dlsend, dlall, bacc, slope_s, tsend, tin, rsend, rin, rall, rsum, acc,
            send, recv, wsem):
     me_p = lax.axis_index("dp")
     me_m = lax.axis_index("mp")
@@ -75,8 +76,14 @@
 
     load_wi = pltpu.make_async_copy(w_in, wi, wsem.at[0])
     load_wo = pltpu.make_async_copy(w_out, wo, wsem.at[1])
-    load_wi.start()
-    load_wo.start()
+    load_tok = pltpu.make_async_copy(tok_in, tok, wsem.at[2])
+    load_cot = pltpu.make_async_copy(cot_in, cot, wsem.at[3])
+    load_grp = pltpu.make_async_copy(grp_in, grp, wsem.at[4])
+    load_rt = pltpu.make_async_copy(rt_in, rt, wsem.at[5])
+    load_tok.start()
+    load_grp.start()
+    load_rt.start()
+    load_cot.start()
 
     bar = pltpu.get_barrier_semaphore()
 
@@ -118,10 +125,16 @@
             return c
         lax.fori_loop(1, NMP, body, 0)
 
+    load_tok.wait()
     blocks(tok, xs)
     pl.semaphore_wait(bar, 31 + 7)
     send_row(xs, xin, S_X, R_X)
+    load_cot.wait()
     blocks(cot, cs)
+    load_wi.start()
+    load_wo.start()
+    load_grp.wait()
+    load_rt.wait()
     xin[me_p] = xs[me_p]
     cin[me_p] = cs[me_p]
 
@@ -282,7 +295,7 @@
     sig = 1.0 / (1.0 + jnp.exp(-pre))
     act_f = pre * sig
     slope = sig * (1.0 + pre * (1.0 - sig))
-    dtok[:, 0:256] = slope
+    slope_s[...] = slope
     active = act_f.astype(BF)
     parts(active, wo, pb, sb, S_PSIB, R_PSIB)
     pair_sums(pb, sb, xsum, xr, R_PSIB, S_PX, R_PX)
@@ -290,7 +303,7 @@
         quad_forward(g_back, R_BX, S_BF, R_BF, j)
     for j in range(CH):
         project(g_back, cf, wo, R_BSIB, R_BF, j)
-    d_pre_f = acc[...] * dtok[:, 0:256]
+    d_pre_f = acc[...] * slope_s[...]
     d_pre = d_pre_f.astype(BF)
     first = (pb, sb, xr, rb, pin, R_PX, S_PA, R_PA)
     second = (pb2, sb2, xr2, rb2, din, R_DX, S_DA, R_DA)
@@ -326,13 +339,17 @@
     oin[me_p] = osend[me_p]
 
     wait_bytes(din.at[pl.ds(0, 63)], recv.at[R_DA])
-    for h in range(2):
-        bacc[...] += dot_nt(half(din, h, 512), half(xin, h, 256))
+    back_rows = [half(din, h, 512) for h in range(2)]
+    for h in range(2):
+        bacc[...] += dot_nt(back_rows[h], half(xin, h, 256))
     wlsend[...] = jnp.sum(bacc[...].reshape(64, 8, 256) * m8[None], axis=1).reshape(8, 8, 256)
     send_col(wlsend, wlin, S_DW, R_DW, True)
     wlin[me_m] = wlsend[me_m]
     for h in range(2):
-        dtok[:, h * 256:(h + 1) * 256] = dot_tn(amat[...], half(din, h, 512))
+        res = dot_tn(amat[...], back_rows[h])
+        gsend[:, h * 8:(h + 1) * 8, :] = res.reshape(32, 8, 256).astype(BF)
+    send_row(gsend, gin, S_G, R_G)
+    gin[me_p] = gsend[me_p]
     wait_bytes(wlin.at[pl.ds(0, 7)], recv.at[R_DW])
     d_weight = jnp.sum(wlin[...], axis=0)
     prod = mix_own * d_weight
@@ -348,41 +365,76 @@
     wait_bytes(dlall.at[pl.ds(0, 7)], recv.at[R_DL])
     dl = jnp.concatenate([half(dlall, 0, 64), half(dlall, 1, 64)], axis=1)
     for h in range(2):
-        part = dot(dl, half(xin, h, 256))
-        for k in range(2):
-            tile = part[:, k * 128:(k + 1) * 128].reshape(8, 8, 128)
-            for e in range(8):
-                rsend[e * 4 + h * 2 + k] = tile[e]
-    send_row(rsend, rin, S_R, R_R)
-    rin[me_p] = rsend[me_p]
-    for h in range(2):
-        res = dtok[:, h * 256:(h + 1) * 256] + dot_tn(dl, rt[:, h * 256:(h + 1) * 256])
-        gsend[:, h * 8:(h + 1) * 8, :] = res.reshape(32, 8, 256).astype(BF)
-    send_row(gsend, gin, S_G, R_G)
-    gin[me_p] = gsend[me_p]
-    def place(src, out):
-        for h in range(2):
-            res = dot_tn(perm, half(src, h, 256)).astype(BF)
-            out[:, :, h * 256:(h + 1) * 256] = res.reshape(4, 64, 256)
+        part = dot(dl, half(xin, h, 256)).astype(BF)
+        for e in range(4):
+            for k in range(2):
+                rsend[e * 4 + h * 2 + k] = part[e * 16:(e + 1) * 16, k * 128:(k + 1) * 128]
+    unit = (iota((64, 128), 0) == iota((64, 128), 1)).astype(F32).astype(BF)
+    reducer = me_p % 2 == 0
+    mine = me_p // 2
+
+    def send_tile(k, c):
+        peer = (mine + k) % 16
+        rcopy(rsend.at[peer], rin.at[me_p], S_R, R_R, (peer * 2, me_m)).start()
+        return c
+    lax.fori_loop(1, 16, send_tile, 0)
+
+    @pl.when(me_p % 2 == 1)
+    def _():
+        rcopy(rsend.at[mine], rin.at[me_p], S_R, R_R, (mine * 2, me_m)).start()
+
+    tsend[...] = dot_tn(dl, unit).reshape(32, 8, 128)
+    send_row(tsend, tin, S_T, R_T)
+    tin[me_p] = tsend[me_p]
+
+    def place(src, h):
+        return dot_tn(perm, half(src, h, 256))
 
     wait_bytes(oin.at[pl.ds(0, 31)], recv.at[R_O])
-    place(oin, o_mix)
-    wait_bytes(rin.at[pl.ds(0, 31)], recv.at[R_R])
-    rsum[...] = jnp.sum(rin[...], axis=0)
-
-    def share(k, c):
-        peer = (me_p + k) % NDP
-        rcopy(rsum, rall.at[me_p], S_RG, R_RG, (peer, me_m)).start()
-        return c
-    lax.fori_loop(1, NDP, share, 0)
-    rall[me_p] = rsum[...]
-
+    for h in range(2):
+        o_mix[:, :, h * 256:(h + 1) * 256] = place(oin, h).reshape(4, 64, 256).astype(BF)
+
+    @pl.when(reducer)
+    def _():
+        rin[me_p] = rsend[mine]
+        wait_bytes(rin.at[pl.ds(0, 31)], recv.at[R_R])
+        total = jnp.sum(rin[...].astype(F32), axis=0).astype(BF)
+        rsum[...] = total
+        rall[mine] = total
+
+        def share(k, c):
+            rcopy(rsum, rall.at[mine], S_RG, R_RG, ((me_p + k) % NDP, me_m)).start()
+            return c
+        lax.fori_loop(1, NDP, share, 0)
+
+    wait_bytes(tin.at[pl.ds(0, 31)], recv.at[R_T])
+    d_rows = dot_tn(perm, tin[...].reshape(256, 128).astype(BF)).astype(BF)
     wait_bytes(gin.at[pl.ds(0, 31)], recv.at[R_G])
-    place(gin, o_grad)
-    wait_bytes(rall.at[pl.ds(0, 31)], recv.at[R_RG])
-    for e in range(8):
+    for h in range(2):
+        cols = slice(h * 256, (h + 1) * 256)
+        res = place(gin, h) + dot(d_rows[:, 0:64], rt[:, cols])
+        o_grad[:, :, cols] = res.reshape(4, 64, 256).astype(BF)
+
+    @pl.when(reducer)
+    def _():
+        wait_bytes(rall.at[pl.ds(0, 15)], recv.at[R_RG])
+
+    @pl.when(me_p % 2 == 1)
+    def _():
+        wait_bytes(rall, recv.at[R_RG])
+
+    for e in range(4):
         for k in range(4):
-            o_router[e * 8:(e + 1) * 8, k * 128:(k + 1) * 128] = rall[e * 4 + k]
+            o_router[e * 16:(e + 1) * 16, k * 128:(k + 1) * 128] = rall[e * 4 + k].astype(F32)
+
+    @pl.when(me_p % 2 == 1)
+    def _():
+        wait_bytes(rsend, send.at[S_R])
+
+    @pl.when(reducer)
+    def _():
+        wait_bytes(rsend.at[pl.ds(0, 15)], send.at[S_R])
+        wait_bytes(rin.at[pl.ds(0, 31)], send.at[S_RG])
 
     for view, s in (
         (xs.at[pl.ds(0, 31)], S_X), (cs.at[pl.ds(0, 31)], S_C), (lin.at[pl.ds(0, 7)], S_L),
@@ -392,7 +444,7 @@
         (sb, S_PSIB), (xsum, S_PX), (rb.at[pl.ds(0, 63)], S_PA),
         (sb2, S_DSIB), (xsum2, S_DX), (rb2.at[pl.ds(0, 63)], S_DA),
         (osend.at[pl.ds(0, 31)], S_O), (wlin.at[pl.ds(0, 7)], S_DW), (dlall.at[pl.ds(0, 7)], S_DL),
-        (gsend.at[pl.ds(0, 31)], S_G), (rsend.at[pl.ds(0, 31)], S_R), (rall.at[pl.ds(0, 31)], S_RG),
+        (gsend.at[pl.ds(0, 31)], S_G), (tsend.at[pl.ds(0, 31)], S_T),
     ):
         wait_bytes(view, send.at[s])
 
@@ -410,6 +462,7 @@
     vm = lambda shape, dt=BF: pltpu.VMEM(shape, dt)
     blk32, blk64 = (32, 16, 256), (64, 16, 256)
     scratch = [
+        vm((4, 64, 512)), vm((4, 64, 512)), vm((2, 128), jnp.int32), vm((64, 512)),
         vm(blk32), vm(blk32), vm(blk32), vm(blk32),
         vm((8, 8, 256), F32), vm((8, 8, 256), F32), vm((16, 128)), vm((8, 16, 128)), vm((512, 256)),
         vm(blk64), vm(blk64),
@@ -418,11 +471,11 @@
         vm((4,) + blk64), vm((2,) + blk64), vm(blk64), vm(blk64), vm(blk64), vm(blk64),
         vm((4,) + blk64), vm((2,) + blk64), vm(blk64), vm(blk64), vm(blk64), vm(blk64),
         vm(blk32), vm(blk32), vm(blk32), vm(blk32),
-        vm((8, 8, 256), F32), vm((8, 8, 256), F32), vm((16, 128)), vm((8, 16, 128)), vm((512, 256), F32), vm((256, 512), F32),
-        vm((32, 8, 128), F32), vm((32, 8, 128), F32), vm((32, 8, 128), F32), vm((8, 128), F32),
+        vm((8, 8, 256), F32), vm((8, 8, 256), F32), vm((16, 128)), vm((8, 16, 128)), vm((512, 256), F32), vm((256, 256), F32),
+        vm((32, 8, 128), F32), vm((32, 8, 128), F32), vm((16, 16, 128)), vm((32, 16, 128)), vm((16, 16, 128)), vm((16, 128)),
         vm((256, 256), F32),
         pltpu.SemaphoreType.DMA((N_SEND,)), pltpu.SemaphoreType.DMA((N_RECV,)),
-        pltpu.SemaphoreType.DMA((2,)),
+        pltpu.SemaphoreType.DMA((6,)),
     ]
     in_vmem = pl.BlockSpec(memory_space=pltpu.VMEM)
     anywhere = pl.BlockSpec(memory_space=pl.ANY)
@@ -437,13 +490,14 @@
     results = pl.pallas_call(
         kernel,
         out_shape=shapes,
-        in_specs=[in_vmem, in_vmem, in_vmem, in_vmem, in_hbm, in_hbm],
+        in_specs=[in_hbm] * 6,
         out_specs=[in_vmem] * 5,
         scratch_shapes=scratch,
         compiler_params=pltpu.CompilerParams(
-            collective_id=0, has_side_effects=True, vmem_limit_bytes=48 * 1024 * 1024),
+            collective_id=0, has_side_effects=True, vmem_limit_bytes=44 * 1024 * 1024),
         cost_estimate=pl.CostEstimate(flops=4 * 10**9, bytes_accessed=10**7, transcendentals=10**5),
-    )(tokens, cotangent, groups, router.T, w_in, w_out)
+    )(*[pltpu.with_memory_space_constraint(a, pltpu.HBM)
+        for a in (tokens, cotangent, groups, router.T, w_in, w_out)])
     mixed_out, tokens_grad, router_t, g_in, g_out = pl.pallas_call(
         copy_out,
         out_shape=shapes,

time: 131 us -> 127 us (0.969)
  local copies, waits for them, and re-layouts: 3.41 us -> 0 us
    unnamed x8 -> x0, local copies, waits for them, and re-layouts: 3.41 us -> none
where the time goes in v4:
time: 127 us
  Pallas kernels  126 us (99%)
    pallas_call x1, Pallas kernels, per_device(): pl.pallas_call(kernel, out_shape=shapes, in_specs=[in_hbm] * 6, out_specs...  124 us

profile of v4, /device:TPU:1, one launch (start us, length us, event | category | flops | bytes accessed | tf_op | source)
XLA Modules:
  0.0 127.1 jit_solution(17918640296464794445)
XLA Ops:
  0.6 124.2 %shard_map.101 = (bf16[4,64,512]{2,1,0:T(8,128)(2,1)S(1)}, bf16[4,64,512]{2,1,0:T(8,128)(2,1)S(1)}, f32[64,512]{1,0:T(8,128)S(1)}, bf16[256,4096]{1,0:T(8,128)(2,1)S(1)}, bf16[256,4096]{1,0:T(8,128)(2,1)S(1)}) custom-call(bf16[4,64,512]{2,1,0:T(8,128)(2,1)} %tok_in.1, bf16[4,64,512]{2,1,0:T(8,128)(2,1)} %cot_in.1, s32[2,128]{1,0:T(2,128)} %grp_in.1, ...), custom_call_target="tpu_custom_call" | custom-call | flops 4000000000 | bytes 10000000 | tf_op jit(solution)/shard_map/pallas_call | solution.py:490
  124.9 2.2 %shard_map.102 = (bf16[4,64,512]{2,1,0:T(8,128)(2,1)}, bf16[4,64,512]{2,1,0:T(8,128)(2,1)}, f32[64,512]{1,0:T(8,128)}, bf16[256,4096]{1,0:T(8,128)(2,1)}, bf16[256,4096]{1,0:T(8,128)(2,1)}) custom-call(bf16[4,64,512]{2,1,0:T(8,128)(2,1)S(1)} %get-tuple-element.15.refs_0_, bf16[4,64,512]{2,1,0:T(8,128)(2,1)S(1)} %get-tuple-element.16.refs_1_, ...), custom_call_target="tpu_custom_call" | custom-call | tf_op jit(solution)/shard_map/pallas_call | solution.py:501

commit v5 on v4

--- a/solution.py
+++ b/solution.py
@@ -10,7 +10,7 @@
 F32 = jnp.float32
 NDP = 32
 NMP = 8
-CH = 4
+CH = 8
 
 NT = (((1,), (1,)), ((), ()))
 TN = (((0,), (0,)), ((), ()))
@@ -40,9 +40,9 @@
 S_PSIB, S_PX, S_PA, S_DSIB, S_DX, S_DA, S_O, S_DW, S_DL, S_G, S_R, S_RG, S_T = range(12, 25)
 N_SEND = 25
 R_X, R_C, R_L, R_MIX, R_PA, R_DA, R_O, R_DW, R_DL, R_G, R_R, R_RG = range(12)
-(R_M, R_B, R_QSIB, R_QX, R_QF, R_BSIB, R_BX, R_BF, R_PSIB, R_PX, R_DSIB, R_DX) = range(12, 60, 4)
-R_T = 60
-N_RECV = 61
+(R_M, R_B, R_QSIB, R_QX, R_QF, R_BSIB, R_BX, R_BF, R_PSIB, R_PX, R_DSIB, R_DX) = range(12, 108, 8)
+R_T = 108
+N_RECV = 109
 
 
 def kernel(tok_in, cot_in, grp_in, rt_in, w_in, w_out,
@@ -191,87 +191,73 @@
         dst[q, u] = buf[u]
 
     def send_chunk(src, dst, s, r, j):
+        m = (me_m + j) % NMP
+
         def body(k, c):
-            m = (me_m + 2 * j + k // 8) % NMP
             quad = (p4 + k) % 8
             rcopy(src.at[m * 8 + quad], dst.at[near_q(quad), u], s, r + j, (near_dp(quad), m)).start()
             return c
-        lax.fori_loop(1 if j == 0 else 0, 16, body, 0)
-
-    def chunk_spans(j):
-        return [pl.ds(((me_m - 2 * j - i + NMP) % NMP) * 8, 8) for i in range(2)]
+        lax.fori_loop(1 if j == 0 else 0, 8, body, 0)
+
+    def chunk_span(j):
+        return pl.ds(((me_m - j + NMP) % NMP) * 8, 8)
 
     def quad_chunk(g, r_own, s_sib, r_sib, s_x, r_x, j):
-        wait_bytes(g.at[0, pl.ds(0, 15 if j == 0 else 16)], recv.at[r_own + j])
-        for span in chunk_spans(j):
-            part = g.at[q, span]
-            rcopy(part, part, s_x, r_x + j, (xnb, me_m)).start()
-        for span in chunk_spans(j):
-            part = g.at[q, span]
-            rcopy(part, part, s_sib, r_sib + j, (sib, me_m)).start()
+        wait_bytes(g.at[0, pl.ds(0, 7 if j == 0 else 8)], recv.at[r_own + j])
+        part = g.at[q, chunk_span(j)]
+        rcopy(part, part, s_x, r_x + j, (xnb, me_m)).start()
+        rcopy(part, part, s_sib, r_sib + j, (sib, me_m)).start()
 
     def quad_forward(g, r_x, s_f, r_f, j):
-        wait_bytes(g.at[0, pl.ds(0, 16)], recv.at[r_x + j])
-        for span in chunk_spans(j):
-            part = g.at[q_x, span]
-            rcopy(part, part, s_f, r_f + j, (sib, me_m)).start()
+        part = g.at[q_x, chunk_span(j)]
+        wait_bytes(part, recv.at[r_x + j])
+        rcopy(part, part, s_f, r_f + j, (sib, me_m)).start()
 
     def project(g, flat, w, r_sib, r_f, j):
-        wait_bytes(g.at[0, pl.ds(0, 16)], recv.at[r_sib + j])
-        wait_bytes(g.at[0, pl.ds(0, 16)], recv.at[r_f + j])
-        if j == 0:
-            acc[...] = jnp.zeros((256, 256), F32)
-
-        def body(i, c):
-            m = (me_m - 2 * j - i + NMP) % NMP
+        m = (me_m - j + NMP) % NMP
+        wait_bytes(g.at[0, pl.ds(0, 8)], recv.at[r_sib + j])
+        wait_bytes(g.at[0, pl.ds(0, 8)], recv.at[r_f + j])
+        for h in range(2):
+            col = pl.multiple_of(m * 512 + h * 256, 256)
+            part = g[:, pl.ds(m * 8, 8), h * 8:(h + 1) * 8, :].astype(F32).reshape(256, 256).astype(BF)
+            flat[:, pl.ds(col, 256)] = part
+            res = dot_nt(part, w[:, pl.ds(col, 256)])
+            if j == 0 and h == 0:
+                acc[...] = res
+            else:
+                acc[...] += res
+
+    def parts(rows, w, buf, landing, s, r):
+        def chunk(j, c):
+            m = (me_m + j) % NMP
             for h in range(2):
                 col = pl.multiple_of(m * 512 + h * 256, 256)
-                part = g[:, pl.ds(m * 8, 8), h * 8:(h + 1) * 8, :].astype(F32).reshape(256, 256).astype(BF)
-                flat[:, pl.ds(col, 256)] = part
-                acc[...] += dot_nt(part, w[:, pl.ds(col, 256)])
-            return c
-        lax.fori_loop(0, 2, body, 0)
-
-    def parts(rows, w, buf, landing, s, r):
-        def chunk(j, c):
-            jj = (me_m // 2 + j) % CH
-
-            def one(i, c2):
-                m = jj * 2 + i
-                for h in range(2):
-                    col = pl.multiple_of(m * 512 + h * 256, 256)
-                    res = dot(rows, w[:, pl.ds(col, 256)])
-                    buf[:, pl.ds(m * 8, 8), h * 8:(h + 1) * 8, :] = res.reshape(4, 8, 8, 256).astype(BF)
-                return c2
-            lax.fori_loop(0, 2, one, 0)
-            span = pl.ds(jj * 16, 16)
+                res = dot(rows, w[:, pl.ds(col, 256)])
+                buf[:, pl.ds(m * 8, 8), h * 8:(h + 1) * 8, :] = res.reshape(4, 8, 8, 256).astype(BF)
+            span = pl.ds(m * 8, 8)
             rcopy(buf.at[q_d, span], landing.at[1, span], s, r + j, (sib, me_m)).start()
             rcopy(buf.at[q_sib, span], landing.at[0, span], s, r + j, (sib, me_m)).start()
             return c
         lax.fori_loop(0, CH, chunk, 0)
 
-    def pair_sums(buf, landing, out, far, r_sib, s, r):
-        def chunk(j, c):
-            jj = (me_m // 2 + j) % CH
-            span = pl.ds(jj * 16, 16)
-            wait_bytes(landing.at[pl.ds(0, 2), span], recv.at[r_sib + j])
-            out[span] = (buf[q_x, span].astype(F32) + landing[1, span].astype(F32)).astype(BF)
-            rcopy(out.at[span], far.at[span], s, r + j, (xnb, me_m)).start()
-            return c
-        lax.fori_loop(0, CH, chunk, 0)
+    def pair_sum(buf, landing, out, far, r_sib, s, r, j):
+        span = pl.ds(((me_m + j) % NMP) * 8, 8)
+        wait_bytes(landing.at[pl.ds(0, 2), span], recv.at[r_sib + j])
+        out[span] = (buf[q_x, span].astype(F32) + landing[1, span].astype(F32)).astype(BF)
+        rcopy(out.at[span], far.at[span], s, r + j, (xnb, me_m)).start()
 
     def total_chunk(buf, landing, far, out, home, r_x, s, r, j):
-        jj = (me_m // 2 + j) % CH
-        span = pl.ds(jj * 16, 16)
+        m = (me_m + j) % NMP
+        span = pl.ds(m * 8, 8)
         wait_bytes(far.at[span], recv.at[r_x + j])
         out[span] = (buf[q, span].astype(F32) + landing[0, span].astype(F32)
                      + far[span].astype(F32)).astype(BF)
 
         def post(k, c):
-            v = jj * 16 + (u + k) % 16
-            rcopy(out.at[v], home.at[u], s, r, (near_dp(v % 8), v // 8)).start()
-            return c
-        lax.fori_loop(1 if j == 0 else 0, 16, post, 0)
+            quad = (p4 + k) % 8
+            rcopy(out.at[m * 8 + quad], home.at[u], s, r, (near_dp(quad), m)).start()
+            return c
+        lax.fori_loop(1 if j == 0 else 0, 8, post, 0)
         if j == 0:
             home[u] = out[u]
 
@@ -289,39 +275,41 @@
     load_wi.wait()
     load_wo.wait()
     for j in range(CH):
-        quad_chunk(g_back, R_B, S_BSIB, R_BSIB, S_BX, R_BX, j)
         project(g_fwd, xf, wi, R_QSIB, R_QF, j)
     pre = acc[...]
     sig = 1.0 / (1.0 + jnp.exp(-pre))
     act_f = pre * sig
-    slope = sig * (1.0 + pre * (1.0 - sig))
-    slope_s[...] = slope
+    slope_s[...] = sig * (1.0 + pre * (1.0 - sig))
     active = act_f.astype(BF)
+    active_t = act_f.T.astype(BF)
     parts(active, wo, pb, sb, S_PSIB, R_PSIB)
-    pair_sums(pb, sb, xsum, xr, R_PSIB, S_PX, R_PX)
+    first = (pb, sb, xr, rb, pin, R_PX, S_PA, R_PA)
+    second = (pb2, sb2, xr2, rb2, din, R_DX, S_DA, R_DA)
     for j in range(CH):
-        quad_forward(g_back, R_BX, S_BF, R_BF, j)
-    for j in range(CH):
-        project(g_back, cf, wo, R_BSIB, R_BF, j)
+        quad_chunk(g_back, R_B, S_BSIB, R_BSIB, S_BX, R_BX, j)
+        pair_sum(pb, sb, xsum, xr, R_PSIB, S_PX, R_PX, j)
+        if j > 0:
+            quad_forward(g_back, R_BX, S_BF, R_BF, j - 1)
+            total_chunk(*first, j - 1)
+            project(g_back, cf, wo, R_BSIB, R_BF, j - 1)
+    quad_forward(g_back, R_BX, S_BF, R_BF, CH - 1)
+    project(g_back, cf, wo, R_BSIB, R_BF, CH - 1)
     d_pre_f = acc[...] * slope_s[...]
     d_pre = d_pre_f.astype(BF)
-    first = (pb, sb, xr, rb, pin, R_PX, S_PA, R_PA)
-    second = (pb2, sb2, xr2, rb2, din, R_DX, S_DA, R_DA)
-    total_chunk(*first, 0)
-    total_chunk(*first, 1)
     parts(d_pre, wi, pb2, sb2, S_DSIB, R_DSIB)
-    total_chunk(*first, 2)
-    pair_sums(pb2, sb2, xsum2, xr2, R_DSIB, S_DX, R_DX)
-    total_chunk(*first, 3)
-    active_t = act_f.T.astype(BF)
+    for j in range(CH):
+        pair_sum(pb2, sb2, xsum2, xr2, R_DSIB, S_DX, R_DX, j)
+    total_chunk(*first, CH - 1)
     d_pre_t = d_pre_f.T.astype(BF)
 
-    def weight_grads(m, c):
-        col = pl.ds(pl.multiple_of(m * 512, 512), 512)
-        o_wout[:, col] = dot(active_t, cf[:, col]).astype(BF)
-        o_win[:, col] = dot(d_pre_t, xf[:, col]).astype(BF)
-        return c
-    lax.fori_loop(0, NMP, weight_grads, 0)
+    def weight_grad(out, lhs, rhs):
+        def body(m, c):
+            col = pl.ds(pl.multiple_of(m * 512, 512), 512)
+            out[:, col] = dot(lhs, rhs[:, col]).astype(BF)
+            return c
+        lax.fori_loop(0, NMP, body, 0)
+
+    weight_grad(o_wout, active_t, cf)
     for j in range(CH):
         total_chunk(*second, j)
 
@@ -337,6 +325,8 @@
             bacc[...] += part
     send_row(osend, oin, S_O, R_O)
     oin[me_p] = osend[me_p]
+
+    weight_grad(o_win, d_pre_t, xf)
 
     wait_bytes(din.at[pl.ds(0, 63)], recv.at[R_DA])
     back_rows = [half(din, h, 512) for h in range(2)]

time: 127 us -> 134 us (1.055)
  Pallas kernels: 126 us -> 133 us
    pallas_call x1, Pallas kernels: 124 us -> 131 us  [per_device(): pl.pallas_call(kernel, out_shape=shapes, in_specs=[in_hbm] * 6, out_specs...]
where the time goes in v5:
time: 134 us
  Pallas kernels  133 us (99%)
    pallas_call x1, Pallas kernels, per_device(): pl.pallas_call(kernel, out_shape=shapes, in_specs=[in_hbm] * 6, out_specs...  131 us

profile of v5, /device:TPU:1, one launch (start us, length us, event | category | flops | bytes accessed | tf_op | source)
XLA Modules:
  0.0 133.7 jit_solution(13001613817704936625)
XLA Ops:
  0.6 130.8 %shard_map.101 = (bf16[4,64,512]{2,1,0:T(8,128)(2,1)S(1)}, bf16[4,64,512]{2,1,0:T(8,128)(2,1)S(1)}, f32[64,512]{1,0:T(8,128)S(1)}, bf16[256,4096]{1,0:T(8,128)(2,1)S(1)}, bf16[256,4096]{1,0:T(8,128)(2,1)S(1)}) custom-call(bf16[4,64,512]{2,1,0:T(8,128)(2,1)} %tok_in.1, bf16[4,64,512]{2,1,0:T(8,128)(2,1)} %cot_in.1, s32[2,128]{1,0:T(2,128)} %grp_in.1, ...), custom_call_target="tpu_custom_call" | custom-call | flops 4000000000 | bytes 10000000 | tf_op jit(solution)/shard_map/pallas_call | solution.py:480
  131.4 2.2 %shard_map.102 = (bf16[4,64,512]{2,1,0:T(8,128)(2,1)}, bf16[4,64,512]{2,1,0:T(8,128)(2,1)}, f32[64,512]{1,0:T(8,128)}, bf16[256,4096]{1,0:T(8,128)(2,1)}, bf16[256,4096]{1,0:T(8,128)(2,1)}) custom-call(bf16[4,64,512]{2,1,0:T(8,128)(2,1)S(1)} %get-tuple-element.15.refs_0_, bf16[4,64,512]{2,1,0:T(8,128)(2,1)S(1)} %get-tuple-element.16.refs_1_, ...), custom_call_target="tpu_custom_call" | custom-call | tf_op jit(solution)/shard_map/pallas_call | solution.py:491

commit v6 on v5

--- a/solution.py
+++ b/solution.py
@@ -37,12 +37,11 @@
 
 
 (S_X, S_C, S_L, S_MIX, S_M, S_B, S_QSIB, S_QX, S_QF, S_BSIB, S_BX, S_BF) = range(12)
-S_PSIB, S_PX, S_PA, S_DSIB, S_DX, S_DA, S_O, S_DW, S_DL, S_G, S_R, S_RG, S_T = range(12, 25)
-N_SEND = 25
+S_PSIB, S_PX, S_PA, S_DSIB, S_DX, S_DA, S_O, S_DW, S_DL, S_G, S_R, S_RG = range(12, 24)
+N_SEND = 24
 R_X, R_C, R_L, R_MIX, R_PA, R_DA, R_O, R_DW, R_DL, R_G, R_R, R_RG = range(12)
 (R_M, R_B, R_QSIB, R_QX, R_QF, R_BSIB, R_BX, R_BF, R_PSIB, R_PX, R_DSIB, R_DX) = range(12, 108, 8)
-R_T = 108
-N_RECV = 109
+N_RECV = 108
 
 
 def kernel(tok_in, cot_in, grp_in, rt_in, w_in, w_out,
@@ -50,7 +49,7 @@
            tok, cot, grp, rt, xs, cs, xin, cin, lsend, lin, mixsend, mixall, amat, mbuf, bbuf,
            g_fwd, g_back, xf, cf, wi, wo, pb, sb, xsum, xr, rb, pin,
            pb2, sb2, xsum2, xr2, rb2, din, osend, oin, gsend, gin,
-           wlsend, wlin, dlsend, dlall, bacc, slope_s, tsend, tin, rsend, rin, rall, rsum, acc,
+           wlsend, wlin, dlsend, dlall, bacc, slope_s, rows_s, rows2_s, lhs_s, lhs2_s, rsend, rin, rall, rsum, acc,
            send, recv, wsem):
     me_p = lax.axis_index("dp")
     me_m = lax.axis_index("mp")
@@ -110,12 +109,12 @@
             res = dot(perm, rows[:, h * 256:(h + 1) * 256])
             out[:, h * 8:(h + 1) * 8, :] = res.reshape(32, 8, 256).astype(BF)
 
-    def send_row(src, dst, s, r):
+    def send_row(src, dst, s, r, low=1, high=NDP):
         def body(k, c):
             peer = (me_p + k) % NDP
             rcopy(src.at[peer], dst.at[me_p], s, r, (peer, me_m)).start()
             return c
-        lax.fori_loop(1, NDP, body, 0)
+        lax.fori_loop(low, high, body, 0)
 
     def send_col(src, dst, s, r, spread):
         def body(k, c):
@@ -131,6 +130,7 @@
     send_row(xs, xin, S_X, R_X)
     load_cot.wait()
     blocks(cot, cs)
+    send_row(cs, cin, S_C, R_C)
     load_wi.start()
     load_wo.start()
     load_grp.wait()
@@ -156,7 +156,6 @@
     r0, r1 = rt[:, 0:256], rt[:, 256:512]
     lsend[...] = (dot_nt(r0, x0) + dot_nt(r1, x1)).reshape(8, 8, 256)
     send_col(lsend, lin, S_L, R_L, True)
-    send_row(cs, cin, S_C, R_C)
     lin[me_m] = lsend[me_m]
     wait_bytes(lin.at[pl.ds(0, 7)], recv.at[R_L])
     logit = jnp.sum(lin[...], axis=0)
@@ -227,18 +226,15 @@
             else:
                 acc[...] += res
 
-    def parts(rows, w, buf, landing, s, r):
-        def chunk(j, c):
-            m = (me_m + j) % NMP
-            for h in range(2):
-                col = pl.multiple_of(m * 512 + h * 256, 256)
-                res = dot(rows, w[:, pl.ds(col, 256)])
-                buf[:, pl.ds(m * 8, 8), h * 8:(h + 1) * 8, :] = res.reshape(4, 8, 8, 256).astype(BF)
-            span = pl.ds(m * 8, 8)
-            rcopy(buf.at[q_d, span], landing.at[1, span], s, r + j, (sib, me_m)).start()
-            rcopy(buf.at[q_sib, span], landing.at[0, span], s, r + j, (sib, me_m)).start()
-            return c
-        lax.fori_loop(0, CH, chunk, 0)
+    def part_chunk(rows, w, buf, landing, s, r, j):
+        m = (me_m + j) % NMP
+        for h in range(2):
+            col = pl.multiple_of(m * 512 + h * 256, 256)
+            res = dot(rows, w[:, pl.ds(col, 256)])
+            buf[:, pl.ds(m * 8, 8), h * 8:(h + 1) * 8, :] = res.reshape(4, 8, 8, 256).astype(BF)
+        span = pl.ds(m * 8, 8)
+        rcopy(buf.at[q_d, span], landing.at[1, span], s, r + j, (sib, me_m)).start()
+        rcopy(buf.at[q_sib, span], landing.at[0, span], s, r + j, (sib, me_m)).start()
 
     def pair_sum(buf, landing, out, far, r_sib, s, r, j):
         span = pl.ds(((me_m + j) % NMP) * 8, 8)
@@ -266,52 +262,142 @@
         send_chunk(mbuf, g_fwd, S_M, R_M, j)
     wait_bytes(cin.at[pl.ds(0, 31)], recv.at[R_C])
     mixing((half(cin, 0, 256), half(cin, 1, 256)), bbuf, g_back)
-    for j in range(CH):
-        quad_chunk(g_fwd, R_M, S_QSIB, R_QSIB, S_QX, R_QX, j)
-        send_chunk(bbuf, g_back, S_B, R_B, j)
-        if j > 0:
-            quad_forward(g_fwd, R_QX, S_QF, R_QF, j - 1)
-    quad_forward(g_fwd, R_QX, S_QF, R_QF, CH - 1)
+    def weight_grad(out, lhs, rhs, m):
+        out[:, m * 512:(m + 1) * 512] = dot(lhs[...], rhs[:, m * 512:(m + 1) * 512]).astype(BF)
+
     load_wi.wait()
     load_wo.wait()
-    for j in range(CH):
-        project(g_fwd, xf, wi, R_QSIB, R_QF, j)
+    first = (pb, sb, xr, rb, pin, R_PX, S_PA, R_PA)
+    second = (pb2, sb2, xr2, rb2, din, R_DX, S_DA, R_DA)
+    quad_chunk(g_fwd, R_M, S_QSIB, R_QSIB, S_QX, R_QX, 0)
+    send_chunk(bbuf, g_back, S_B, R_B, 0)
+    quad_chunk(g_fwd, R_M, S_QSIB, R_QSIB, S_QX, R_QX, 1)
+    send_chunk(bbuf, g_back, S_B, R_B, 1)
+    quad_forward(g_fwd, R_QX, S_QF, R_QF, 0)
+    quad_chunk(g_fwd, R_M, S_QSIB, R_QSIB, S_QX, R_QX, 2)
+    send_chunk(bbuf, g_back, S_B, R_B, 2)
+    quad_forward(g_fwd, R_QX, S_QF, R_QF, 1)
+    project(g_fwd, xf, wi, R_QSIB, R_QF, 0)
+    quad_chunk(g_fwd, R_M, S_QSIB, R_QSIB, S_QX, R_QX, 3)
+    send_chunk(bbuf, g_back, S_B, R_B, 3)
+    quad_forward(g_fwd, R_QX, S_QF, R_QF, 2)
+    project(g_fwd, xf, wi, R_QSIB, R_QF, 1)
+    quad_chunk(g_fwd, R_M, S_QSIB, R_QSIB, S_QX, R_QX, 4)
+    send_chunk(bbuf, g_back, S_B, R_B, 4)
+    quad_forward(g_fwd, R_QX, S_QF, R_QF, 3)
+    project(g_fwd, xf, wi, R_QSIB, R_QF, 2)
+    quad_chunk(g_fwd, R_M, S_QSIB, R_QSIB, S_QX, R_QX, 5)
+    send_chunk(bbuf, g_back, S_B, R_B, 5)
+    quad_forward(g_fwd, R_QX, S_QF, R_QF, 4)
+    project(g_fwd, xf, wi, R_QSIB, R_QF, 3)
+    quad_chunk(g_fwd, R_M, S_QSIB, R_QSIB, S_QX, R_QX, 6)
+    send_chunk(bbuf, g_back, S_B, R_B, 6)
+    quad_forward(g_fwd, R_QX, S_QF, R_QF, 5)
+    project(g_fwd, xf, wi, R_QSIB, R_QF, 4)
+    quad_chunk(g_fwd, R_M, S_QSIB, R_QSIB, S_QX, R_QX, 7)
+    send_chunk(bbuf, g_back, S_B, R_B, 7)
+    quad_forward(g_fwd, R_QX, S_QF, R_QF, 6)
+    project(g_fwd, xf, wi, R_QSIB, R_QF, 5)
+    quad_forward(g_fwd, R_QX, S_QF, R_QF, 7)
+    quad_chunk(g_back, R_B, S_BSIB, R_BSIB, S_BX, R_BX, 0)
+    project(g_fwd, xf, wi, R_QSIB, R_QF, 6)
+    quad_chunk(g_back, R_B, S_BSIB, R_BSIB, S_BX, R_BX, 1)
+    project(g_fwd, xf, wi, R_QSIB, R_QF, 7)
+    quad_chunk(g_back, R_B, S_BSIB, R_BSIB, S_BX, R_BX, 2)
     pre = acc[...]
     sig = 1.0 / (1.0 + jnp.exp(-pre))
     act_f = pre * sig
     slope_s[...] = sig * (1.0 + pre * (1.0 - sig))
-    active = act_f.astype(BF)
-    active_t = act_f.T.astype(BF)
-    parts(active, wo, pb, sb, S_PSIB, R_PSIB)
-    first = (pb, sb, xr, rb, pin, R_PX, S_PA, R_PA)
-    second = (pb2, sb2, xr2, rb2, din, R_DX, S_DA, R_DA)
-    for j in range(CH):
-        quad_chunk(g_back, R_B, S_BSIB, R_BSIB, S_BX, R_BX, j)
-        pair_sum(pb, sb, xsum, xr, R_PSIB, S_PX, R_PX, j)
-        if j > 0:
-            quad_forward(g_back, R_BX, S_BF, R_BF, j - 1)
-            total_chunk(*first, j - 1)
-            project(g_back, cf, wo, R_BSIB, R_BF, j - 1)
-    quad_forward(g_back, R_BX, S_BF, R_BF, CH - 1)
-    project(g_back, cf, wo, R_BSIB, R_BF, CH - 1)
+    rows_s[...] = act_f.astype(BF)
+    lhs_s[...] = act_f.T.astype(BF)
+    part_chunk(rows_s[...], wo, pb, sb, S_PSIB, R_PSIB, 0)
+    part_chunk(rows_s[...], wo, pb, sb, S_PSIB, R_PSIB, 1)
+    quad_chunk(g_back, R_B, S_BSIB, R_BSIB, S_BX, R_BX, 3)
+    quad_forward(g_back, R_BX, S_BF, R_BF, 0)
+    part_chunk(rows_s[...], wo, pb, sb, S_PSIB, R_PSIB, 2)
+    part_chunk(rows_s[...], wo, pb, sb, S_PSIB, R_PSIB, 3)
+    quad_chunk(g_back, R_B, S_BSIB, R_BSIB, S_BX, R_BX, 4)
+    quad_forward(g_back, R_BX, S_BF, R_BF, 1)
+    part_chunk(rows_s[...], wo, pb, sb, S_PSIB, R_PSIB, 4)
+    part_chunk(rows_s[...], wo, pb, sb, S_PSIB, R_PSIB, 5)
+    quad_chunk(g_back, R_B, S_BSIB, R_BSIB, S_BX, R_BX, 5)
+    quad_forward(g_back, R_BX, S_BF, R_BF, 2)
+    project(g_back, cf, wo, R_BSIB, R_BF, 0)
+    part_chunk(rows_s[...], wo, pb, sb, S_PSIB, R_PSIB, 6)
+    part_chunk(rows_s[...], wo, pb, sb, S_PSIB, R_PSIB, 7)
+    quad_chunk(g_back, R_B, S_BSIB, R_BSIB, S_BX, R_BX, 6)
+    quad_forward(g_back, R_BX, S_BF, R_BF, 3)
+    project(g_back, cf, wo, R_BSIB, R_BF, 1)
+    quad_chunk(g_back, R_B, S_BSIB, R_BSIB, S_BX, R_BX, 7)
+    pair_sum(pb, sb, xsum, xr, R_PSIB, S_PX, R_PX, 0)
+    pair_sum(pb, sb, xsum, xr, R_PSIB, S_PX, R_PX, 1)
+    pair_sum(pb, sb, xsum, xr, R_PSIB, S_PX, R_PX, 2)
+    pair_sum(pb, sb, xsum, xr, R_PSIB, S_PX, R_PX, 3)
+    pair_sum(pb, sb, xsum, xr, R_PSIB, S_PX, R_PX, 4)
+    pair_sum(pb, sb, xsum, xr, R_PSIB, S_PX, R_PX, 5)
+    pair_sum(pb, sb, xsum, xr, R_PSIB, S_PX, R_PX, 6)
+    pair_sum(pb, sb, xsum, xr, R_PSIB, S_PX, R_PX, 7)
+    quad_forward(g_back, R_BX, S_BF, R_BF, 4)
+    project(g_back, cf, wo, R_BSIB, R_BF, 2)
+    quad_forward(g_back, R_BX, S_BF, R_BF, 5)
+    project(g_back, cf, wo, R_BSIB, R_BF, 3)
+    quad_forward(g_back, R_BX, S_BF, R_BF, 6)
+    project(g_back, cf, wo, R_BSIB, R_BF, 4)
+    quad_forward(g_back, R_BX, S_BF, R_BF, 7)
+    project(g_back, cf, wo, R_BSIB, R_BF, 5)
+    project(g_back, cf, wo, R_BSIB, R_BF, 6)
+    project(g_back, cf, wo, R_BSIB, R_BF, 7)
     d_pre_f = acc[...] * slope_s[...]
-    d_pre = d_pre_f.astype(BF)
-    parts(d_pre, wi, pb2, sb2, S_DSIB, R_DSIB)
-    for j in range(CH):
-        pair_sum(pb2, sb2, xsum2, xr2, R_DSIB, S_DX, R_DX, j)
-    total_chunk(*first, CH - 1)
-    d_pre_t = d_pre_f.T.astype(BF)
-
-    def weight_grad(out, lhs, rhs):
-        def body(m, c):
-            col = pl.ds(pl.multiple_of(m * 512, 512), 512)
-            out[:, col] = dot(lhs, rhs[:, col]).astype(BF)
-            return c
-        lax.fori_loop(0, NMP, body, 0)
-
-    weight_grad(o_wout, active_t, cf)
-    for j in range(CH):
-        total_chunk(*second, j)
+    rows2_s[...] = d_pre_f.astype(BF)
+    lhs2_s[...] = d_pre_f.T.astype(BF)
+    total_chunk(*first, 0)
+    part_chunk(rows2_s[...], wi, pb2, sb2, S_DSIB, R_DSIB, 0)
+    weight_grad(o_wout, lhs_s, cf, 0)
+    total_chunk(*first, 1)
+    part_chunk(rows2_s[...], wi, pb2, sb2, S_DSIB, R_DSIB, 1)
+    weight_grad(o_wout, lhs_s, cf, 1)
+    total_chunk(*first, 2)
+    part_chunk(rows2_s[...], wi, pb2, sb2, S_DSIB, R_DSIB, 2)
+    pair_sum(pb2, sb2, xsum2, xr2, R_DSIB, S_DX, R_DX, 0)
+    weight_grad(o_wout, lhs_s, cf, 2)
+    total_chunk(*first, 3)
+    part_chunk(rows2_s[...], wi, pb2, sb2, S_DSIB, R_DSIB, 3)
+    pair_sum(pb2, sb2, xsum2, xr2, R_DSIB, S_DX, R_DX, 1)
+    weight_grad(o_wout, lhs_s, cf, 3)
+    total_chunk(*first, 4)
+    part_chunk(rows2_s[...], wi, pb2, sb2, S_DSIB, R_DSIB, 4)
+    pair_sum(pb2, sb2, xsum2, xr2, R_DSIB, S_DX, R_DX, 2)
+    weight_grad(o_wout, lhs_s, cf, 4)
+    total_chunk(*first, 5)
+    part_chunk(rows2_s[...], wi, pb2, sb2, S_DSIB, R_DSIB, 5)
+    pair_sum(pb2, sb2, xsum2, xr2, R_DSIB, S_DX, R_DX, 3)
+    weight_grad(o_wout, lhs_s, cf, 5)
+    total_chunk(*first, 6)
+    part_chunk(rows2_s[...], wi, pb2, sb2, S_DSIB, R_DSIB, 6)
+    pair_sum(pb2, sb2, xsum2, xr2, R_DSIB, S_DX, R_DX, 4)
+    weight_grad(o_wout, lhs_s, cf, 6)
+    total_chunk(*first, 7)
+    part_chunk(rows2_s[...], wi, pb2, sb2, S_DSIB, R_DSIB, 7)
+    pair_sum(pb2, sb2, xsum2, xr2, R_DSIB, S_DX, R_DX, 5)
+    weight_grad(o_wout, lhs_s, cf, 7)
+    pair_sum(pb2, sb2, xsum2, xr2, R_DSIB, S_DX, R_DX, 6)
+    pair_sum(pb2, sb2, xsum2, xr2, R_DSIB, S_DX, R_DX, 7)
+    total_chunk(*second, 0)
+    weight_grad(o_win, lhs2_s, xf, 0)
+    total_chunk(*second, 1)
+    weight_grad(o_win, lhs2_s, xf, 1)
+    total_chunk(*second, 2)
+    weight_grad(o_win, lhs2_s, xf, 2)
+    total_chunk(*second, 3)
+    weight_grad(o_win, lhs2_s, xf, 3)
+    total_chunk(*second, 4)
+    weight_grad(o_win, lhs2_s, xf, 4)
+    total_chunk(*second, 5)
+    weight_grad(o_win, lhs2_s, xf, 5)
+    total_chunk(*second, 6)
+    weight_grad(o_win, lhs2_s, xf, 6)
+    total_chunk(*second, 7)
+    weight_grad(o_win, lhs2_s, xf, 7)
 
     wait_bytes(pin.at[pl.ds(0, 63)], recv.at[R_PA])
     for h in range(2):
@@ -323,10 +409,7 @@
             bacc[...] = part
         else:
             bacc[...] += part
-    send_row(osend, oin, S_O, R_O)
     oin[me_p] = osend[me_p]
-
-    weight_grad(o_win, d_pre_t, xf)
 
     wait_bytes(din.at[pl.ds(0, 63)], recv.at[R_DA])
     back_rows = [half(din, h, 512) for h in range(2)]
@@ -335,11 +418,9 @@
     wlsend[...] = jnp.sum(bacc[...].reshape(64, 8, 256) * m8[None], axis=1).reshape(8, 8, 256)
     send_col(wlsend, wlin, S_DW, R_DW, True)
     wlin[me_m] = wlsend[me_m]
-    for h in range(2):
-        res = dot_tn(amat[...], back_rows[h])
-        gsend[:, h * 8:(h + 1) * 8, :] = res.reshape(32, 8, 256).astype(BF)
-    send_row(gsend, gin, S_G, R_G)
-    gin[me_p] = gsend[me_p]
+    send_row(osend, oin, S_O, R_O, 1, 16)
+    for h in range(2):
+        bacc[h * 256:(h + 1) * 256, :] = dot_tn(amat[...], back_rows[h])
     wait_bytes(wlin.at[pl.ds(0, 7)], recv.at[R_DW])
     d_weight = jnp.sum(wlin[...], axis=0)
     prod = mix_own * d_weight
@@ -351,6 +432,7 @@
     dlsend[0:8, :] = d_logit[:, 0:128].astype(BF)
     dlsend[8:16, :] = d_logit[:, 128:256].astype(BF)
     send_col(dlsend, dlall, S_DL, R_DL, False)
+    send_row(osend, oin, S_O, R_O, 16, NDP)
     dlall[me_m] = dlsend[...]
     wait_bytes(dlall.at[pl.ds(0, 7)], recv.at[R_DL])
     dl = jnp.concatenate([half(dlall, 0, 64), half(dlall, 1, 64)], axis=1)
@@ -359,7 +441,6 @@
         for e in range(4):
             for k in range(2):
                 rsend[e * 4 + h * 2 + k] = part[e * 16:(e + 1) * 16, k * 128:(k + 1) * 128]
-    unit = (iota((64, 128), 0) == iota((64, 128), 1)).astype(F32).astype(BF)
     reducer = me_p % 2 == 0
     mine = me_p // 2
 
@@ -373,9 +454,11 @@
     def _():
         rcopy(rsend.at[mine], rin.at[me_p], S_R, R_R, (mine * 2, me_m)).start()
 
-    tsend[...] = dot_tn(dl, unit).reshape(32, 8, 128)
-    send_row(tsend, tin, S_T, R_T)
-    tin[me_p] = tsend[me_p]
+    for h in range(2):
+        res = bacc[h * 256:(h + 1) * 256, :] + dot_tn(dl, rt[:, h * 256:(h + 1) * 256])
+        gsend[:, h * 8:(h + 1) * 8, :] = res.reshape(32, 8, 256).astype(BF)
+    send_row(gsend, gin, S_G, R_G, 1, 16)
+    gin[me_p] = gsend[me_p]
 
     def place(src, h):
         return dot_tn(perm, half(src, h, 256))
@@ -397,13 +480,11 @@
             return c
         lax.fori_loop(1, NDP, share, 0)
 
-    wait_bytes(tin.at[pl.ds(0, 31)], recv.at[R_T])
-    d_rows = dot_tn(perm, tin[...].reshape(256, 128).astype(BF)).astype(BF)
+    send_row(gsend, gin, S_G, R_G, 16, NDP)
     wait_bytes(gin.at[pl.ds(0, 31)], recv.at[R_G])
     for h in range(2):
         cols = slice(h * 256, (h + 1) * 256)
-        res = place(gin, h) + dot(d_rows[:, 0:64], rt[:, cols])
-        o_grad[:, :, cols] = res.reshape(4, 64, 256).astype(BF)
+        o_grad[:, :, cols] = place(gin, h).reshape(4, 64, 256).astype(BF)
 
     @pl.when(reducer)
     def _():
@@ -434,7 +515,7 @@
         (sb, S_PSIB), (xsum, S_PX), (rb.at[pl.ds(0, 63)], S_PA),
         (sb2, S_DSIB), (xsum2, S_DX), (rb2.at[pl.ds(0, 63)], S_DA),
         (osend.at[pl.ds(0, 31)], S_O), (wlin.at[pl.ds(0, 7)], S_DW), (dlall.at[pl.ds(0, 7)], S_DL),
-        (gsend.at[pl.ds(0, 31)], S_G), (tsend.at[pl.ds(0, 31)], S_T),
+        (gsend.at[pl.ds(0, 31)], S_G),
     ):
         wait_bytes(view, send.at[s])
 
@@ -462,7 +543,8 @@
         vm((4,) + blk64), vm((2,) + blk64), vm(blk64), vm(blk64), vm(blk64), vm(blk64),
         vm(blk32), vm(blk32), vm(blk32), vm(blk32),
         vm((8, 8, 256), F32), vm((8, 8, 256), F32), vm((16, 128)), vm((8, 16, 128)), vm((512, 256), F32), vm((256, 256), F32),
-        vm((32, 8, 128), F32), vm((32, 8, 128), F32), vm((16, 16, 128)), vm((32, 16, 128)), vm((16, 16, 128)), vm((16, 128)),
+        vm((256, 256)), vm((256, 256)), vm((256, 256)), vm((256, 256)),
+        vm((16, 16, 128)), vm((32, 16, 128)), vm((16, 16, 128)), vm((16, 128)),
         vm((256, 256), F32),
         pltpu.SemaphoreType.DMA((N_SEND,)), pltpu.SemaphoreType.DMA((N_RECV,)),
         pltpu.SemaphoreType.DMA((6,)),

time: 134 us -> 125 us (0.933)
  Pallas kernels: 133 us -> 124 us
    pallas_call x1, Pallas kernels: 131 us -> 122 us  [per_device(): pl.pallas_call(kernel, out_shape=shapes, in_specs=[in_hbm] * 6, out_specs...]
where the time goes in v6:
time: 125 us
  Pallas kernels  124 us (99%)
    pallas_call x1, Pallas kernels, per_device(): pl.pallas_call(kernel, out_shape=shapes, in_specs=[in_hbm] * 6, out_specs...  122 us

profile of v6, /device:TPU:1, one launch (start us, length us, event | category | flops | bytes accessed | tf_op | source)
XLA Modules:
  0.0 125.0 jit_solution(157650465464164193)
XLA Ops:
  0.6 122.1 %shard_map.101 = (bf16[4,64,512]{2,1,0:T(8,128)(2,1)S(1)}, bf16[4,64,512]{2,1,0:T(8,128)(2,1)S(1)}, f32[64,512]{1,0:T(8,128)S(1)}, bf16[256,4096]{1,0:T(8,128)(2,1)S(1)}, bf16[256,4096]{1,0:T(8,128)(2,1)S(1)}) custom-call(bf16[4,64,512]{2,1,0:T(8,128)(2,1)} %tok_in.1, bf16[4,64,512]{2,1,0:T(8,128)(2,1)} %cot_in.1, s32[2,128]{1,0:T(2,128)} %grp_in.1, ...), custom_call_target="tpu_custom_call" | custom-call | flops 4000000000 | bytes 10000000 | tf_op jit(solution)/shard_map/pallas_call | solution.py:562
  122.8 2.2 %shard_map.102 = (bf16[4,64,512]{2,1,0:T(8,128)(2,1)}, bf16[4,64,512]{2,1,0:T(8,128)(2,1)}, f32[64,512]{1,0:T(8,128)}, bf16[256,4096]{1,0:T(8,128)(2,1)}, bf16[256,4096]{1,0:T(8,128)(2,1)}) custom-call(bf16[4,64,512]{2,1,0:T(8,128)(2,1)S(1)} %get-tuple-element.15.refs_0_, bf16[4,64,512]{2,1,0:T(8,128)(2,1)S(1)} %get-tuple-element.16.refs_1_, ...), custom_call_target="tpu_custom_call" | custom-call | tf_op jit(solution)/shard_map/pallas_call | solution.py:573

commit v7 on v6

--- a/solution.py
+++ b/solution.py
@@ -463,10 +463,6 @@
     def place(src, h):
         return dot_tn(perm, half(src, h, 256))
 
-    wait_bytes(oin.at[pl.ds(0, 31)], recv.at[R_O])
-    for h in range(2):
-        o_mix[:, :, h * 256:(h + 1) * 256] = place(oin, h).reshape(4, 64, 256).astype(BF)
-
     @pl.when(reducer)
     def _():
         rin[me_p] = rsend[mine]
@@ -481,6 +477,11 @@
         lax.fori_loop(1, NDP, share, 0)
 
     send_row(gsend, gin, S_G, R_G, 16, NDP)
+
+    wait_bytes(oin.at[pl.ds(0, 31)], recv.at[R_O])
+    for h in range(2):
+        o_mix[:, :, h * 256:(h + 1) * 256] = place(oin, h).reshape(4, 64, 256).astype(BF)
+
     wait_bytes(gin.at[pl.ds(0, 31)], recv.at[R_G])
     for h in range(2):
         cols = slice(h * 256, (h + 1) * 256)

time: 125 us -> 125 us (level)
  no operation moved by 1% of the time
where the time goes in v7:
time: 125 us
  Pallas kernels  124 us (99%)
    pallas_call x1, Pallas kernels, per_device(): pl.pallas_call(kernel, out_shape=shapes, in_specs=[in_hbm] * 6, out_specs...  122 us

profile of v7, /device:TPU:1, one launch (start us, length us, event | category | flops | bytes accessed | tf_op | source)
XLA Modules:
  0.0 124.7 jit_solution(14219686938804575085)
XLA Ops:
  0.6 121.8 %shard_map.101 = (bf16[4,64,512]{2,1,0:T(8,128)(2,1)S(1)}, bf16[4,64,512]{2,1,0:T(8,128)(2,1)S(1)}, f32[64,512]{1,0:T(8,128)S(1)}, bf16[256,4096]{1,0:T(8,128)(2,1)S(1)}, bf16[256,4096]{1,0:T(8,128)(2,1)S(1)}) custom-call(bf16[4,64,512]{2,1,0:T(8,128)(2,1)} %tok_in.1, bf16[4,64,512]{2,1,0:T(8,128)(2,1)} %cot_in.1, s32[2,128]{1,0:T(2,128)} %grp_in.1, ...), custom_call_target="tpu_custom_call" | custom-call | flops 4000000000 | bytes 10000000 | tf_op jit(solution)/shard_map/pallas_call | solution.py:563
  122.4 2.2 %shard_map.102 = (bf16[4,64,512]{2,1,0:T(8,128)(2,1)}, bf16[4,64,512]{2,1,0:T(8,128)(2,1)}, f32[64,512]{1,0:T(8,128)}, bf16[256,4096]{1,0:T(8,128)(2,1)}, bf16[256,4096]{1,0:T(8,128)(2,1)}) custom-call(bf16[4,64,512]{2,1,0:T(8,128)(2,1)S(1)} %get-tuple-element.15.refs_0_, bf16[4,64,512]{2,1,0:T(8,128)(2,1)S(1)} %get-tuple-element.16.refs_1_, ...), custom_call_target="tpu_custom_call" | custom-call | tf_op jit(solution)/shard_map/pallas_call | solution.py:574
